TPU v7x, 256 devices: a whole 4x4x8 slice. The times are simulated.
256 devices in a mesh: group: 32 (over z, x), tensor: 8 (over y, core).
Axes of the slice: x: 4, y: 4, z: 8, core: 2. Of those that a mesh axis runs over, the one named last changes fastest.
Arguments:
- hidden: bfloat16 [8192, 7168], P('group', 'tensor'), may hold values from -6 to 6
- w_kv_a: bfloat16 [7168, 576], P('tensor'), may hold values from -0.0625 to 0.0625
- kv_gain: float32 [512], replicated, may hold values from 0.5 to 1.5
- q_latent: bfloat16 [8192, 1536], P('group'), may hold values from -6 to 6
- w_q_b: bfloat16 [1536, 12288], P(None, 'tensor'), may hold values from -0.15625 to 0.15625
- w_key_up: bfloat16 [512, 8192], P(None, 'tensor'), may hold values from -0.5 to 0.5
- w_value_up: bfloat16 [512, 8192], P(None, 'tensor'), may hold values from -0.25 to 0.25
- pool: bfloat16 [4096, 32, 576], P('group', 'tensor'), may hold values from -170 to 170
- page_table: int32 [32, 64], replicated, may hold values from 0 to 4095, as said below
- prefix_len: int32 [32], replicated, may hold values from 32 to 2048, as said below
- decode_owner: int32 [32], replicated, may hold values from 0 to 31, each once
Outputs:
- attn_out: bfloat16 [8192, 8192], P('group', 'tensor')
- decode_pages: bfloat16 [8192, 576], P(('group', 'tensor'))
Inputs may be any that keep to these rules, and one draw needn't show every extreme that they name: `page_table`: each row names every owner group (page id // 128) exactly 2 times; no page id appears twice in the whole table. `prefix_len`: the largest value is reached in every draw. `decode_owner`: a permutation of the groups.
All inputs are finite; a program needn't handle non-finite values.
Results may differ from a plain program's by a relative error of at most 0.012.
Values may be sent and summed in bfloat16 or wider, within the bound.
No kernel may reach another device: no remote copies, remote signals or barrier semaphores. Data moves between devices by JAX's collectives and lax.ppermute only.
A program may use at most 128 MiB of HBM per device.

v0:
```python
import jax
import jax.numpy as jnp
from jax import lax
from jax.sharding import PartitionSpec as P

NOPE = 128
ROPE = 64
VDIM = 128
KVR = 512
CAP = 2


rope_base = 50000.0
masked_value = -1e30


def apply_rope(values, positions):
    half_width = values.shape[-1] // 2
    frequency = rope_base ** (-2.0 * jnp.arange(half_width, dtype=jnp.float32) / values.shape[-1])
    angles = positions.astype(jnp.float32)[:, None] * frequency[None, :]
    angles = angles.reshape(angles.shape[:1] + (1,) * (values.ndim - 2) + angles.shape[1:])
    cosine = jnp.cos(angles)
    sine = jnp.sin(angles)
    first = values[..., :half_width]
    second = values[..., half_width:]
    return jnp.concatenate(
        [first * cosine - second * sine, second * cosine + first * sine], axis=-1
    )


def finish_latent(projected, positions, kv_gain):
    nope_part = projected[:, :KVR]
    mean_square = jnp.mean(nope_part * nope_part, axis=-1, keepdims=True)
    normed = nope_part * lax.rsqrt(mean_square + 1e-06) * kv_gain
    rotated = apply_rope(projected[:, KVR:], positions)
    return jnp.concatenate([normed, rotated], axis=-1).astype(jnp.bfloat16)


def shards(
    hidden,
    w_kv_a,
    kv_gain,
    q_latent,
    w_q_b,
    w_key_up,
    w_value_up,
    pool,
    page_table,
    prefix_len,
    decode_owner,
):
    groups = lax.axis_size("group")
    tensors = lax.axis_size("tensor")
    group_index = lax.axis_index("group")
    tensor_index = lax.axis_index("tensor")
    new_tokens = hidden.shape[0]
    share_rows = new_tokens // tensors
    latent_width = w_kv_a.shape[1]
    heads_here = w_key_up.shape[1] // NOPE
    slot_count = pool.shape[0]
    page_rows = pool.shape[1]
    max_pages = page_table.shape[1]
    scale = float(NOPE + ROPE) ** (-0.5)
    my_length = prefix_len[group_index]
    positions = my_length + jnp.arange(new_tokens, dtype=jnp.int32)
    partial_sum = jnp.dot(hidden, w_kv_a, preferred_element_type=jnp.float32)
    summed = lax.psum(partial_sum, "tensor")
    new_latent = finish_latent(summed, positions, kv_gain)
    own_share = lax.dynamic_slice_in_dim(new_latent, tensor_index * share_rows, share_rows, 0)
    group_ids = jnp.arange(groups, dtype=jnp.int32)
    segment = lax.all_gather(own_share, "group", axis=0, tiled=True)
    count = segment.shape[0] // share_rows
    blocks = segment.reshape(count, share_rows, latent_width)
    sources = jnp.arange(count, dtype=jnp.int32)
    owners = jnp.sum(
        jnp.where(sources[:, None] == group_ids[None, :], decode_owner[None, :], 0), axis=1
    )
    chosen = jnp.where((owners == group_index)[:, None, None], blocks.astype(jnp.float32), 0.0)
    pushed = jnp.sum(chosen, axis=0)
    decode_pages = pushed.astype(jnp.bfloat16)
    q_full = jnp.dot(q_latent, w_q_b, preferred_element_type=jnp.float32).reshape(
        new_tokens, heads_here, NOPE + ROPE
    )
    q_nope = q_full[..., :NOPE].astype(jnp.bfloat16)
    q_rope = apply_rope(q_full[..., NOPE:], positions).astype(jnp.bfloat16)
    key_up = w_key_up.reshape(KVR, heads_here, NOPE)
    absorbed = jnp.einsum(
        "nhd,chd->nhc", q_nope, key_up, preferred_element_type=jnp.float32
    ).astype(jnp.bfloat16)
    query_rows = jnp.concatenate([absorbed, q_rope], axis=-1).reshape(
        new_tokens * heads_here, latent_width
    )
    owner_table = page_table // slot_count
    slot_table = page_table % slot_count
    page_ids = jnp.arange(max_pages, dtype=jnp.int32)
    same_owner = owner_table[:, :, None] == owner_table[:, None, :]
    earlier = page_ids[None, :] < page_ids[:, None]
    page_rank = jnp.sum(jnp.logical_and(same_owner, earlier[None]), axis=2)
    rank_slots = jnp.arange(CAP, dtype=jnp.int32)
    wanted = jnp.logical_and(
        (owner_table == group_index)[:, :, None], page_rank[:, :, None] == rank_slots[None, None, :]
    )
    picked = jnp.sum(jnp.where(wanted, slot_table[:, :, None], 0), axis=1)
    outgoing = pool[picked]
    incoming = lax.all_to_all(outgoing, "group", split_axis=0, concat_axis=0, tiled=True)
    flattened = incoming.reshape(groups * CAP, page_rows, latent_width)
    position = owner_table[group_index] * CAP + page_rank[group_index]
    own_pages = flattened[position]
    contract_last = (((1,), (1,)), ((), ()))
    gathered = lax.all_gather(own_pages, "tensor", axis=1, tiled=True)
    key_rows = gathered.reshape(max_pages * page_rows * tensors, latent_width)
    raw_scores = (
        lax.dot_general(key_rows, query_rows, contract_last, preferred_element_type=jnp.float32)
        * scale
    )
    key_pos = jnp.arange(key_rows.shape[0], dtype=jnp.int32)
    prefix_scores = jnp.where((key_pos < my_length)[:, None], raw_scores, masked_value)
    new_raw = (
        lax.dot_general(new_latent, query_rows, contract_last, preferred_element_type=jnp.float32)
        * scale
    )
    query_token = jnp.arange(new_tokens * heads_here, dtype=jnp.int32) // heads_here
    causal = jnp.arange(new_tokens, dtype=jnp.int32)[:, None] <= query_token[None, :]
    new_scores = jnp.where(causal, new_raw, masked_value)
    scores = jnp.concatenate([prefix_scores, new_scores], axis=0)
    row_max = jnp.max(scores, axis=0, keepdims=True)
    expo = jnp.exp(scores - row_max)
    weights = (expo / jnp.sum(expo, axis=0, keepdims=True)).astype(jnp.bfloat16)
    value_rows = jnp.concatenate([key_rows[:, :KVR], new_latent[:, :KVR]], axis=0)
    context = lax.dot_general(
        weights, value_rows, (((0,), (0,)), ((), ())), preferred_element_type=jnp.float32
    )
    context = context.astype(jnp.bfloat16).reshape(new_tokens, heads_here, KVR)
    value_up = w_value_up.reshape(KVR, heads_here, VDIM)
    head_out = jnp.einsum("nhc,chv->nhv", context, value_up, preferred_element_type=jnp.float32)
    attn_out = head_out.astype(jnp.bfloat16).reshape(new_tokens, heads_here * VDIM)
    return (attn_out, decode_pages)


def solution(mesh):
    return jax.shard_map(
        shards,
        mesh=mesh,
        in_specs=(
            P("group", "tensor"),
            P("tensor", None),
            P(),
            P("group", None),
            P(None, "tensor"),
            P(None, "tensor"),
            P(None, "tensor"),
            P("group", "tensor", None),
            P(),
            P(),
            P(),
        ),
        out_specs=(P("group", "tensor"), P(("group", "tensor"), None)),
        check_vma=False,
    )
```

profile of v0, /device:TPU:1, one launch (start us, length us, event | category | flops | bytes accessed | tf_op | source)
XLA Modules:
  0.0 240.2 jit_solution(10830866487319459579)
XLA Ops:
  7.3 2.8 %fusion.38 = f32[256,576]{0,1:T(8,128)} fusion(bf16[256,896]{1,0:T(8,128)(2,1)} %param.11, bf16[896,576]{0,1:T(8,128)(2,1)} %param.12), kind=kOutput, calls=%fused_computation.83 | convolution fusion | flops 264241152 | bytes 2080768 | tf_op jit(solution)/shard_map/dot_general | solution.py:66
  11.3 67.1 %all-reduce.2.cloned.1.call-done = f32[256,576]{0,1:T(8,128)} async-done(((f32[256,576]{0,1:T(8,128)}), f32[256,576]{0,1:T(8,128)}) %all-reduce.2.cloned.1.call-update) | async-done | bytes 589840 | tf_op jit(solution)/shard_map/psum | solution.py:67
  78.4 1.1 multiply_reduce_fusion
  79.5 1.6 subtract_convert_fusion.1
  81.1 1.2 multiply_convert_fusion
  83.3 0.9 convert_reduce_fusion
  85.4 1.6 gather_fusion
  87.0 9.5 %all-to-all-start = ((bf16[32,2,4,576]{3,2,1,0:T(4,128)(2,1)}), bf16[32,2,4,576]{3,2,1,0:T(4,128)(2,1)S(1)}, u32[]{:S(2)}, u32[]{:S(2)}) async-start(bf16[32,2,4,576]{3,2,1,0:T(4,128)(2,1)} %bitcast.2), calls=%async_computation | async-start | bytes 655360 | tf_op jit(solution)/shard_map/all_to_all | solution.py:105
  96.6 11.0 %all-to-all-done = bf16[32,2,4,576]{3,2,1,0:T(4,128)(2,1)S(1)} async-done(((bf16[32,2,4,576]{3,2,1,0:T(4,128)(2,1)}), bf16[32,2,4,576]{3,2,1,0:T(4,128)(2,1)S(1)}, u32[]{:S(2)}, u32[]{:S(2)}) %all-to-all-start) | async-done | bytes 294944 | tf_op jit(solution)/shard_map/all_to_all | solution.py:105
  107.5 0.9 gather_fusion.1
  109.2 4.3 %fusion.37 = f32[256,1536]{0,1:T(8,128)S(1)} fusion(bf16[256,1536]{1,0:T(8,128)(2,1)S(1)} %copy-done.16, bf16[1536,1536]{1,0:T(8,128)(2,1)} %param.15), kind=kOutput, calls=%fused_computation.82 | convolution fusion | flops 1207959552 | bytes 7077888 | tf_op jit(solution)/shard_map/dot_general | solution.py:81
  113.6 1.1 copy-done.4
  114.7 1.3 copy.93
  116.1 1.3 copy.94
  117.4 1.3 copy.92
  118.7 1.1 iota_compare_fusion.4
  121.1 2.0 convert_bitcast_fusion
  124.7 1.5 copy.83
  126.3 1.8 subtract_convert_fusion
  128.6 1.5 copy-done.2
  130.1 3.5 %fusion.36 = (f32[2048]{0:T(1024)S(1)}, f32[256,2048]{1,0:T(8,128)}) fusion(bf16[256,8,576]{2,0,1:T(8,128)(2,1)S(1)} %pad_maximum_fusion, bf16[256,32]{0,1:T(8,128)(2,1)S(1)} %copy-done.10, bf16[256,32]{0,1:T(8,128)(2,1)S(1)} %get-tuple-element.18, bf16[256,512]{0,1:T(8,128)(2,1)S(1)} %multiply_convert_fusion, s32[2048]{0:T(1024)S(1)} %copy-done.12), kind=kOutput, calls=%fused_computation.81 | convolution fusion | flops 606959616 | bytes 4767744 | tf_op jit(solution)/shard_map/dot_general | solution.py:119
  133.6 23.5 %all-gather.4.cloned.1.call-done = bf16[1024,576]{1,0:T(8,128)(2,1)} async-done(((bf16[32,576]{1,0:T(8,128)(2,1)}), bf16[1024,576]{1,0:T(8,128)(2,1)}) %all-gather.4.cloned.1.call-update) | async-done | bytes 1179664 | tf_op jit(solution)/shard_map/all_gather | solution.py:71
  157.0 2.3 fusion.5
  159.3 31.3 %all-gather.6.cloned.1.call-done = bf16[64,32,576]{2,0,1:T(8,128)(2,1)} async-done(((bf16[64,4,576]{2,0,1:T(8,128)(2,1)}), bf16[64,32,576]{2,0,1:T(8,128)(2,1)}) %all-gather.6.cloned.1.call-update) | async-done | bytes 2359312 | tf_op jit(solution)/shard_map/all_gather | solution.py:110
  190.6 3.2 %copy.76 = bf16[64,32,576]{2,1,0:T(8,128)(2,1)S(1)} copy(bf16[64,32,576]{2,0,1:T(8,128)(2,1)} %all-gather.6.cloned.1.call-done) | data formatting | bytes 4718592 | tf_op jit(solution)/shard_map/all_gather | solution.py:110
  194.1 1.6 copy-done.3
  195.6 8.5 %fusion.35 = (f32[2048]{0:T(1024)S(1)}, f32[2048,2048]{1,0:T(8,128)S(1)}) fusion(bf16[2048,576]{1,0:T(8,128)(2,1)S(1)} %bitcast.46, bf16[256,8,576]{2,0,1:T(8,128)(2,1)S(1)} %copy-done.3, pred[2048]{0:T(1024)(128)(4,1)S(1)} %copy-done.14), kind=kOutput, calls=%fused_computation.80 | convolution fusion | flops 4844419072 | bytes 21506048 | tf_op jit(solution)/shard_map/dot_general | solution.py:113
  204.1 5.7 %copy-done.1 = f32[2048,2048]{1,0:T(8,128)} copy-done((f32[2048,2048]{1,0:T(8,128)}, f32[2048,2048]{1,0:T(8,128)S(1)}, u32[]{:S(2)}) %copy-start.1) | copy-done | bytes 16777240
  209.8 6.3 %fusion.1 = f32[2048]{0:T(1024)S(1)} fusion(f32[256,2048]{1,0:T(8,128)} %get-tuple-element.25, f32[2048,2048]{1,0:T(8,128)S(1)} %get-tuple-element.23, f32[2048]{0:T(1024)S(1)} %reduce_max.22), kind=kLoop, calls=%fused_computation.6 | loop fusion | flops 14153728 | bytes 18890752 | tf_op jit(solution)/shard_map/reduce_sum | solution.py:128
  216.1 14.0 %fusion.15 = bf16[256,8,512]{2,1,0:T(8,128)(2,1)} fusion(bf16[256,512]{1,0:T(8,128)(2,1)S(1)} %copy-done.8, bf16[2048,512]{1,0:T(8,128)(2,1)S(1)} %slice.49, f32[256,2048]{1,0:T(8,128)} %get-tuple-element.25, f32[2048,2048]{1,0:T(8,128)} %copy-done.1, f32[2048]{0:T(1024)S(1)} %fusion.1, f32[2048]{0:T(1024)S(1)} %reduce_max.22), kind=kOutput, calls=%fused_computation.25 | convolution fusion | flops 4856479744 | bytes 23347200 | tf_op jit(solution)/shard_map/dot_general | solution.py:130
  230.2 2.5 %fusion.18 = bf16[8,256,128]{1,2,0:T(8,128)(2,1)S(1)} fusion(bf16[512,8,128]{0,2,1:T(8,128)(2,1)S(1)} %bitcast.51, bf16[256,8,512]{2,1,0:T(8,128)(2,1)} %fusion.15), kind=kOutput, calls=%fused_computation.26 | convolution fusion | flops 268697600 | bytes 3670016 | tf_op jit(solution)/shard_map/nhc,chv->nhv/dot_general | solution.py:135
  232.7 1.0 copy.89
  (68 shorter events, 7.8 us)
Async XLA Ops:
  7.2 113.9 %copy-start = (bf16[512,1024]{1,0:T(8,128)(2,1)S(1)}, bf16[512,1024]{1,0:T(8,128)(2,1)}, u32[]{:S(2)}) copy-start(bf16[512,1024]{1,0:T(8,128)(2,1)} %param.16) | copy-start | bytes 3145732
  7.2 3.0 %copy-start.17 = (s32[32]{0:T(128)S(1)}, s32[32]{0:T(128)}, u32[]{:S(2)}) copy-start(s32[32]{0:T(128)} %param.20) | copy-start | bytes 388
  7.2 73.9 %copy-start.13 = (f32[512]{0:T(512)S(1)}, f32[512]{0:T(512)}, u32[]{:S(2)}) copy-start(f32[512]{0:T(512)} %param.13) | copy-start | bytes 6148
  7.2 76.1 %copy-start.11 = (s32[32,64]{1,0:T(8,128)S(1)}, s32[32,64]{1,0:T(8,128)}, u32[]{:S(2)}) copy-start(s32[32,64]{1,0:T(8,128)} %param.19) | copy-start | bytes 24580
  7.2 77.4 %copy-start.7 = (bf16[128,4,576]{0,2,1:T(8,128)(2,1)S(1)}, bf16[128,4,576]{0,2,1:T(8,128)(2,1)}, u32[]{:S(2)}) copy-start(bf16[128,4,576]{0,2,1:T(8,128)(2,1)} %param.18) | copy-start | bytes 1769476
  7.2 71.2 %all-reduce.2.cloned.1.call-start = ((), (), s32[]{:S(2)}) async-start(), calls=%async_computation.1 | async-start | bytes 1179648 | tf_op jit(solution)/shard_map/psum | solution.py:67
  10.1 147.0 %all-gather.4.cloned.1.call-start = ((), (), s32[]{:S(2)}) async-start(), calls=%async_computation.2 | async-start | bytes 1351680 | tf_op jit(solution)/shard_map/all_gather | solution.py:71
  81.1 27.3 %copy-start.9 = (bf16[256,32]{0,1:T(8,128)(2,1)}, bf16[256,32]{0,1:T(8,128)(2,1)S(1)}, u32[]{:S(2)}) copy-start(bf16[256,32]{0,1:T(8,128)(2,1)S(1)} %get-tuple-element.19) | copy-start | bytes 49156
  82.3 26.9 %copy-start.16 = (bf16[256,1536]{1,0:T(8,128)(2,1)S(1)}, bf16[256,1536]{1,0:T(8,128)(2,1)}, u32[]{:S(2)}) copy-start(bf16[256,1536]{1,0:T(8,128)(2,1)} %param.14) | copy-start | bytes 2359300
  87.0 20.6 %all-to-all-start = ((bf16[32,2,4,576]{3,2,1,0:T(4,128)(2,1)}), bf16[32,2,4,576]{3,2,1,0:T(4,128)(2,1)S(1)}, u32[]{:S(2)}, u32[]{:S(2)}) async-start(bf16[32,2,4,576]{3,2,1,0:T(4,128)(2,1)} %bitcast.2), calls=%async_computation | async-start | bytes 655360 | tf_op jit(solution)/shard_map/all_to_all | solution.py:105
  96.5 94.1 %all-gather.6.cloned.1.call-start = ((), (), s32[]{:S(2)}) async-start(), calls=%async_computation.3 | async-start | bytes 2949120 | tf_op jit(solution)/shard_map/all_gather | solution.py:110
  113.5 1.2 copy-start.4
  113.5 3.8 %copy-start.5 = (bf16[512,1024]{1,0:T(8,128)(2,1)S(1)}, bf16[512,1024]{1,0:T(8,128)(2,1)}, u32[]{:S(2)}) copy-start(bf16[512,1024]{1,0:T(8,128)(2,1)} %param.17) | copy-start | bytes 3145732
  114.7 5.7 %copy-start.18 = (s32[32]{0:T(128)S(1)}, s32[32]{0:T(128)}, u32[]{:S(2)}) copy-start(s32[32]{0:T(128)} %param.21) | copy-start | bytes 388
  128.1 2.0 copy-start.10
  128.1 2.0 copy-start.12
  128.6 1.5 copy-start.2
  130.1 27.0 %copy-start.15 = (pred[32]{0:T(512)(128)(4,1)S(1)}, pred[32]{0:T(512)(128)(4,1)}, u32[]{:S(2)}) copy-start(pred[32]{0:T(512)(128)(4,1)} %broadcast_compare_fusion.1) | copy-start | bytes 100
  193.9 1.7 copy-start.3
  193.9 1.7 copy-start.14
  204.1 5.7 %copy-start.1 = (f32[2048,2048]{1,0:T(8,128)}, f32[2048,2048]{1,0:T(8,128)S(1)}, u32[]{:S(2)}) copy-start(f32[2048,2048]{1,0:T(8,128)S(1)} %get-tuple-element.23) | copy-start | bytes 50331652
  209.8 6.3 %copy-start.8 = (bf16[256,512]{1,0:T(8,128)(2,1)S(1)}, bf16[256,512]{1,0:T(8,128)(2,1)}, u32[]{:S(2)}) copy-start(bf16[256,512]{1,0:T(8,128)(2,1)} %copy.85) | copy-start | bytes 786436
  216.1 14.0 %copy-start.6 = (bf16[512,1024]{0,1:T(8,128)(2,1)S(1)}, bf16[512,1024]{0,1:T(8,128)(2,1)}, u32[]{:S(2)}) copy-start(bf16[512,1024]{0,1:T(8,128)(2,1)} %copy.92) | copy-start | bytes 3145732
Sparse Core Ops, SparseCore 0:
  10.4 67.9 all-reduce.1
  83.4 73.6 all-gather.3
  159.5 31.1 all-gather.5
where the time goes:
time: 241 us; the launch traced here: 240 us
  waiting for transfers between devices  133 us (55%)
  matrix products  37.5 us (16%)
  local copies, waits for them, and re-layouts  27.2 us (11%)
  other arithmetic  18.9 us (8%)
  between operations  14.1 us (6%)
  starting transfers between devices  9.66 us (4%)
    psum x1, waiting for transfers between devices, shards(): summed = lax.psum(partial_sum, 'tensor')  67.1 us
    all_gather x1, waiting for transfers between devices, shards(): gathered = lax.all_gather(own_pages, 'tensor', axis=1, tiled=True)  31.3 us
    all_gather x1, waiting for transfers between devices, shards(): segment = lax.all_gather(own_share, 'group', axis=0, tiled=True)  23.5 us
    unnamed x42, local copies, waits for them, and re-layouts  14.4 us
    dot_general x1, matrix products, shards(): lax.dot_general(weights, value_rows, (((0,), (0,)), ((), ())), preferred_...  14 us
    all_to_all x1, waiting for transfers between devices, shards(): lax.all_to_all(outgoing, 'group', split_axis=0, concat_axis=0, tiled=True)  11 us
    all_to_all x1, starting transfers between devices, shards(): lax.all_to_all(outgoing, 'group', split_axis=0, concat_axis=0, tiled=True)  9.54 us
    dot_general x1, matrix products, shards(): lax.dot_general(key_rows, query_rows, contract_last, preferred_element_ty...  8.47 us
  transfers between devices with their start and end apart: 4, of which 4 were waited for; matrix products, arithmetic and copies ran while one was open for 13% of the time, Pallas kernels for 0%

commit v1 on v0

v1 whole, which is shorter than its diff:
```python
import functools

import jax
import jax.numpy as jnp
from jax import lax
from jax.experimental import pallas as pl
from jax.experimental.pallas import tpu as pltpu
from jax.sharding import PartitionSpec as P

NOPE = 128
ROPE = 64
VDIM = 128
KVR = 512
CAP = 2
LAT = KVR + ROPE
WIDE = 640
HALF = ROPE // 2

rope_base = 50000.0
masked_value = -1e30
softmax_scale = float(NOPE + ROPE) ** (-0.5)
log2_scale = softmax_scale * 1.4426950408889634

MIB = 1 << 20
bf16 = jnp.bfloat16
f32 = jnp.float32


def vmem():
    return pl.BlockSpec(memory_space=pltpu.VMEM)


def smem():
    return pl.BlockSpec(memory_space=pltpu.SMEM)


def angle_tables(positions):
    frequency = rope_base ** (-2.0 * jnp.arange(HALF, dtype=f32) / ROPE)
    return positions.astype(f32), frequency


def query_kernel(ql_ref, wq_ref, wk_ref, cos_ref, sin_ref, out_ref):
    q = jnp.dot(ql_ref[...], wq_ref[...], preferred_element_type=f32)
    qt = q.T
    cosine = cos_ref[...]
    sine = sin_ref[...]
    tokens = qt.shape[1]
    for h in range(2):
        base = h * (NOPE + ROPE)
        nope = qt[base:base + NOPE].astype(bf16)
        first = qt[base + NOPE:base + NOPE + HALF]
        second = qt[base + NOPE + HALF:base + NOPE + ROPE]
        absorbed = jnp.dot(wk_ref[:, h * NOPE:(h + 1) * NOPE], nope, preferred_element_type=f32)
        out_ref[h, :KVR, :] = absorbed.astype(bf16)
        out_ref[h, KVR:KVR + HALF, :] = (first * cosine - second * sine).astype(bf16)
        out_ref[h, KVR + HALF:LAT, :] = (second * cosine + first * sine).astype(bf16)
        row = lax.broadcasted_iota(jnp.int32, (WIDE - LAT, tokens), 0)
        out_ref[h, LAT:, :] = jnp.where(row == 0, 1.0, 0.0).astype(bf16)


def make_queries(q_latent, w_q_b, w_key_up, cos_t, sin_t):
    tokens, rank = q_latent.shape
    heads = w_key_up.shape[1] // NOPE
    return pl.pallas_call(
        query_kernel,
        grid=(heads // 2,),
        in_specs=[
            pl.BlockSpec((tokens, rank), lambda i: (0, 0)),
            pl.BlockSpec((rank, 2 * (NOPE + ROPE)), lambda i: (0, i)),
            pl.BlockSpec((KVR, 2 * NOPE), lambda i: (0, i)),
            pl.BlockSpec((HALF, tokens), lambda i: (0, 0)),
            pl.BlockSpec((HALF, tokens), lambda i: (0, 0)),
        ],
        out_specs=pl.BlockSpec((2, WIDE, tokens), lambda i: (i, 0, 0)),
        out_shape=jax.ShapeDtypeStruct((heads, WIDE, tokens), bf16),
        compiler_params=pltpu.CompilerParams(vmem_limit_bytes=32 * MIB),
        cost_estimate=pl.CostEstimate(flops=2 * tokens * rank * heads * 192 + 2 * tokens * KVR * heads * 128,
                                      bytes_accessed=8 * MIB, transcendentals=0),
        name="queries",
    )(q_latent, w_q_b, w_key_up, cos_t, sin_t)


def combine_kernel(y_ref, a_ref, b_ref, own_ref, up_ref, down_ref, far_ref):
    y = y_ref[0]
    rows = own_ref.shape[0]

    def part(d):
        start = pl.multiple_of(lax.rem(y + d, 4) * rows, rows)
        return a_ref[pl.ds(start, rows), :].astype(f32) + b_ref[pl.ds(start, rows), :].astype(f32)

    own_ref[...] = part(0)
    up_ref[...] = part(1).astype(bf16)
    far_ref[...] = part(2).astype(bf16)
    down_ref[...] = part(3).astype(bf16)


def combine(y, a, b):
    rows = a.shape[0] // 4
    return pl.pallas_call(
        combine_kernel,
        in_specs=[smem(), vmem(), vmem()],
        out_specs=[vmem()] * 4,
        out_shape=[jax.ShapeDtypeStruct((rows, LAT), f32)] + [jax.ShapeDtypeStruct((rows, LAT), bf16)] * 3,
        cost_estimate=pl.CostEstimate(flops=a.size, bytes_accessed=8 * a.size, transcendentals=0),
        name="combine",
    )(y, a, b)


def finish_kernel(own_ref, a_ref, b_ref, c_ref, gain_ref, cos_ref, sin_ref, out_ref):
    total = (own_ref[...] + a_ref[...].astype(f32)) + (b_ref[...].astype(f32) + c_ref[...].astype(f32))
    nope = total[:, :KVR]
    mean_square = jnp.mean(nope * nope, axis=-1, keepdims=True)
    out_ref[:, :KVR] = (nope * lax.rsqrt(mean_square + 1e-06) * gain_ref[...]).astype(bf16)
    first = total[:, KVR:KVR + HALF]
    second = total[:, KVR + HALF:LAT]
    cosine = cos_ref[...]
    sine = sin_ref[...]
    rotated = jnp.concatenate([first * cosine - second * sine, second * cosine + first * sine], axis=-1)
    out_ref[:, KVR:LAT] = rotated.astype(bf16)


def finish(own, a, b, c, gain, cosine, sine):
    return pl.pallas_call(
        finish_kernel,
        in_specs=[vmem()] * 7,
        out_specs=vmem(),
        out_shape=jax.ShapeDtypeStruct(own.shape, bf16),
        cost_estimate=pl.CostEstimate(flops=8 * own.size, bytes_accessed=12 * own.size, transcendentals=0),
        name="finish",
    )(own, a, b, c, gain, cosine, sine)


def attention_kernel(blocks, news, first, last, *refs):
    refs = list(refs)
    info_ref = refs.pop(0)
    pos_ref = refs.pop(0)
    qt_ref = refs.pop(0)
    key_refs = [refs.pop(0) for _ in range(blocks)]
    new_refs = [refs.pop(0) for _ in range(news)]
    if not first:
        m_in, l_in, acc_in = refs.pop(0), refs.pop(0), refs.pop(0)
    if last:
        wv_ref = refs.pop(0)
        out_ref = refs.pop(0)
    else:
        m_out, l_out, acc_out = refs.pop(0), refs.pop(0), refs.pop(0)
    keys, values_t = refs
    heads = qt_ref.shape[0]
    tokens = qt_ref.shape[2]
    rows = pos_ref.shape[0]
    lane = lax.broadcasted_iota(jnp.int32, (rows, WIDE - LAT), 1)
    for b in range(blocks):
        here = slice(b * rows, (b + 1) * rows)
        ref = key_refs[b]
        nope = ref[:, :KVR]
        keys[here, :KVR] = nope
        keys[here, KVR:LAT] = ref[:, KVR:LAT]
        out_of_range = jnp.logical_and(pos_ref[...] >= info_ref[b], lane == 0)
        keys[here, LAT:] = jnp.where(out_of_range, masked_value, 0.0).astype(bf16)
        values_t[:, here] = nope.T
    prefix = blocks * rows
    total = prefix
    causal = []
    for b in range(news):
        ref = new_refs[b]
        n = ref.shape[0]
        here = slice(total, total + n)
        nope = ref[...][:, :KVR]
        keys[here, :KVR] = nope
        keys[here, KVR:LAT] = ref[:, KVR:LAT]
        keys[here, LAT:] = jnp.zeros((n, WIDE - LAT), bf16)
        key_token = info_ref[blocks + b] + lax.broadcasted_iota(jnp.int32, (n, tokens), 0)
        causal.append(key_token <= lax.broadcasted_iota(jnp.int32, (n, tokens), 1))
        total += n
    if news:
        values_t[:, prefix:total] = keys[prefix:total, :KVR].T
        allowed = jnp.concatenate(causal, axis=0)
    for h in range(heads):
        s = jnp.dot(keys[...], qt_ref[h], preferred_element_type=f32)
        if news:
            s = jnp.concatenate([s[:prefix], jnp.where(allowed, s[prefix:], masked_value)], axis=0)
        top = jnp.max(s, axis=0, keepdims=True)
        if not first:
            old = m_in[h:h + 1, :]
            top = jnp.maximum(top, old)
        p = jnp.exp2((s - top) * log2_scale)
        norm = jnp.sum(p, axis=0, keepdims=True)
        acc = jnp.dot(values_t[...], p.astype(bf16), preferred_element_type=f32)
        if not first:
            alpha = jnp.exp2((old - top) * log2_scale)
            norm = norm + l_in[h:h + 1, :] * alpha
            acc = acc + acc_in[h] * alpha
        if last:
            context = (acc / norm).astype(bf16)
            head_out = lax.dot_general(
                wv_ref[:, h * VDIM:(h + 1) * VDIM], context, (((0,), (0,)), ((), ())), preferred_element_type=f32
            )
            out_ref[:, h * VDIM:(h + 1) * VDIM] = head_out.T.astype(bf16)
        else:
            m_out[h:h + 1, :] = top
            l_out[h:h + 1, :] = norm
            acc_out[h] = acc


def attention(info, pos, qt, key_blocks, new_blocks, state, w_value_up):
    heads, _, tokens = qt.shape
    first = state is None
    last = w_value_up is not None
    total = sum(b.shape[0] for b in key_blocks) + sum(b.shape[0] for b in new_blocks)
    args = [info, pos, qt, *key_blocks, *new_blocks]
    if not first:
        args += list(state)
    if last:
        args.append(w_value_up)
        out_shape = jax.ShapeDtypeStruct((tokens, heads * VDIM), bf16)
        out_specs = vmem()
    else:
        out_shape = [
            jax.ShapeDtypeStruct((heads, tokens), f32),
            jax.ShapeDtypeStruct((heads, tokens), f32),
            jax.ShapeDtypeStruct((heads, KVR, tokens), f32),
        ]
        out_specs = [vmem()] * 3
    return pl.pallas_call(
        functools.partial(attention_kernel, len(key_blocks), len(new_blocks), first, last),
        in_specs=[smem()] + [vmem()] * (len(args) - 1),
        out_specs=out_specs,
        out_shape=out_shape,
        scratch_shapes=[pltpu.VMEM((total, WIDE), bf16), pltpu.VMEM((KVR, total), bf16)],
        compiler_params=pltpu.CompilerParams(vmem_limit_bytes=40 * MIB),
        cost_estimate=pl.CostEstimate(flops=2 * heads * tokens * total * (WIDE + KVR), bytes_accessed=8 * MIB,
                                      transcendentals=heads * tokens * total),
        name="attention",
    )(*args)


def shards(
    hidden,
    w_kv_a,
    kv_gain,
    q_latent,
    w_q_b,
    w_key_up,
    w_value_up,
    pool,
    page_table,
    prefix_len,
    decode_owner,
):
    groups = lax.axis_size("group")
    group_index = lax.axis_index("group")
    tensor_index = lax.axis_index("tensor")
    y = tensor_index // 2
    core = tensor_index % 2
    new_tokens = hidden.shape[0]
    slot_count = pool.shape[0]
    page_rows = pool.shape[1]
    max_pages = page_table.shape[1]
    my_length = prefix_len[group_index]
    group_ids = jnp.arange(groups, dtype=jnp.int32)

    def tensor_permute(x, step):
        return lax.ppermute(x, "tensor", [(i, step(i)) for i in range(8)])

    up = lambda i: (i + 2) % 8
    down = lambda i: (i - 2) % 8
    far = lambda i: (i + 4) % 8
    other = lambda i: i ^ 1

    owner_table = page_table // slot_count
    page_ids = jnp.arange(max_pages, dtype=jnp.int32)
    code = page_ids[None, :] * slot_count + page_table % slot_count
    mine = owner_table == group_index
    first_code = jnp.min(jnp.where(mine, code, max_pages * slot_count), axis=1)
    last_code = jnp.max(jnp.where(mine, code, -1), axis=1)
    picked = jnp.stack([first_code, last_code], axis=1) % slot_count
    outgoing = pool[picked]
    incoming = lax.all_to_all(outgoing, "group", split_axis=0, concat_axis=0, tiled=True)
    own_block = incoming.reshape(groups * CAP * page_rows, LAT)

    my_owners = owner_table[group_index]
    owned = my_owners[None, :] == group_ids[:, None]
    first_page = jnp.min(jnp.where(owned, page_ids[None, :], max_pages), axis=1)
    last_page = jnp.max(jnp.where(owned, page_ids[None, :], -1), axis=1)
    pages = jnp.stack([first_page, last_page], axis=1)
    row_ids = jnp.arange(page_rows, dtype=jnp.int32)
    pos = (pages[:, :, None] * (page_rows * 8) + row_ids).reshape(-1, 1)

    frequency = rope_base ** (-2.0 * jnp.arange(HALF, dtype=f32) / ROPE)
    positions = (my_length + jnp.arange(new_tokens, dtype=jnp.int32)).astype(f32)
    angles_t = frequency[:, None] * positions[None, :]
    chip_rows = new_tokens // 4
    chip_positions = (my_length + y * chip_rows + jnp.arange(chip_rows, dtype=jnp.int32)).astype(f32)
    angles = chip_positions[:, None] * frequency[None, :]
    partial_sum = jnp.dot(hidden, w_kv_a, preferred_element_type=f32).astype(bf16)
    partner_sum = tensor_permute(partial_sum, other)
    own, to_up, to_down, to_far = combine(y[None], partial_sum, partner_sum)
    from_down = tensor_permute(to_up, up)
    from_up = tensor_permute(to_down, down)
    from_far = tensor_permute(to_far, far)
    latent = finish(own, from_down, from_up, from_far, kv_gain[None, :], jnp.cos(angles), jnp.sin(angles))
    latents = [latent, tensor_permute(latent, up), tensor_permute(latent, down), tensor_permute(latent, far)]
    new_starts = [y, (y + 3) % 4, (y + 1) % 4, (y + 2) % 4]

    share_rows = new_tokens // 8
    share = lax.dynamic_slice_in_dim(latent, core * share_rows, share_rows, 0)
    spread = lax.all_to_all(share[:, None, :], "group", 0, 0, tiled=True)
    source = jnp.sum(jnp.where(decode_owner[None, :] == group_ids[:, None], group_ids[None, :], 0), axis=1)
    decode_pages = lax.all_to_all(spread[source], "group", 0, 0, tiled=True).reshape(share_rows, LAT)

    qt = make_queries(q_latent, w_q_b, w_key_up, jnp.cos(angles_t), jnp.sin(angles_t))

    block_up = tensor_permute(own_block, up)
    block_down = tensor_permute(own_block, down)
    block_far = tensor_permute(own_block, far)
    block_other = tensor_permute(own_block, other)
    block_up_other = tensor_permute(block_up, other)
    block_down_other = tensor_permute(block_down, other)
    block_far_other = tensor_permute(block_far, other)

    def limit(source_tensor):
        return my_length - page_rows * source_tensor

    t = tensor_index
    info1 = jnp.stack([limit(t), limit(t ^ 1)] + [s * chip_rows for s in new_starts])
    state = attention(info1, pos, qt, [own_block, block_other], latents, None, None)
    below, above, across = (t + 6) % 8, (t + 2) % 8, (t + 4) % 8
    info2 = jnp.stack([limit(below), limit(below ^ 1), limit(above), limit(above ^ 1)])
    state = attention(info2, pos, qt, [block_up, block_up_other, block_down, block_down_other], [], state, None)
    info3 = jnp.stack([limit(across), limit(across ^ 1)])
    attn_out = attention(info3, pos, qt, [block_far, block_far_other], [], state, w_value_up)
    return (attn_out, decode_pages)


def solution(mesh):
    return jax.shard_map(
        shards,
        mesh=mesh,
        in_specs=(
            P("group", "tensor"),
            P("tensor", None),
            P(),
            P("group", None),
            P(None, "tensor"),
            P(None, "tensor"),
            P(None, "tensor"),
            P("group", "tensor", None),
            P(),
            P(),
            P(),
        ),
        out_specs=(P("group", "tensor"), P(("group", "tensor"), None)),
        check_vma=False,
    )
```

time: 241 us -> 138 us (0.57)
  waiting for transfers between devices: 133 us -> 18.5 us
  Pallas kernels: 0 us -> 43 us
  matrix products: 37.5 us -> 2.34 us
  starting transfers between devices: 9.66 us -> 44.3 us
  other arithmetic: 18.9 us -> 5.09 us
  local copies, waits for them, and re-layouts: 27.2 us -> 17 us
  between operations: 14.1 us -> 6.92 us
    psum x1 -> x0, waiting for transfers between devices: 67.1 us -> none  [shards(): summed = lax.psum(partial_sum, 'tensor')]
    all_gather x2 -> x0, waiting for transfers between devices: 54.8 us -> none  [the longest x1 31.3 us: shards(): gathered = lax.all_gather(own_pages, 'tensor', axis=1, tiled=True)]
    pallas_call x0 -> x6, Pallas kernels: none -> 43 us  [the longest x3 35 us: attention(): pl.pallas_call(functools.partial(attention_kernel, len(key_blocks), len(n...]
    dot_general x7 -> x1, matrix products: 37.5 us -> 2.34 us  [shards(): jnp.dot(hidden, w_kv_a, preferred_element_type=f32).astype(bf16)]
    ppermute x0 -> x14, starting transfers between devices: none -> 21.4 us  [tensor_permute(): return lax.ppermute(x, 'tensor', [(i, step(i)) for i in range(8)])]
    all_to_all x0 -> x2, waiting for transfers between devices: none -> 16.4 us  [the longest x1 8.39 us: shards(): lax.all_to_all(spread[source], 'group', 0, 0, tiled=True)]
    all_to_all x0 -> x2, starting transfers between devices: none -> 13.5 us  [the longest x1 9.49 us: shards(): spread = lax.all_to_all(share[:, None, :], 'group', 0, 0, tiled=True)]
    all_to_all x1, waiting for transfers between devices: 11 us -> 0.01 us  [shards(): lax.all_to_all(outgoing, 'group', split_axis=0, concat_axis=0, tiled=True)]
  transfers between devices with their start and end apart: 4 -> 17, of which waited for: 4 -> 3; matrix products, arithmetic and copies ran while one was open for 13% -> 10% of each run, Pallas kernels for 0% -> 24%
where the time goes in v1:
time: 138 us; the launch traced here: 137 us
  starting transfers between devices  44.3 us (32%)
  Pallas kernels  43 us (31%)
  waiting for transfers between devices  18.5 us (13%)
  local copies, waits for them, and re-layouts  17 us (12%)
  between operations  6.92 us (5%)
  other arithmetic  5.09 us (4%)
  matrix products  2.34 us (2%)
    pallas_call x3, Pallas kernels, attention(): pl.pallas_call(functools.partial(attention_kernel, len(key_blocks), len(n...  35 us
    ppermute x14, starting transfers between devices, tensor_permute(): return lax.ppermute(x, 'tensor', [(i, step(i)) for i in range(8)])  21.4 us
    unnamed x33, local copies, waits for them, and re-layouts  12.3 us
    all_to_all x1, starting transfers between devices, shards(): spread = lax.all_to_all(share[:, None, :], 'group', 0, 0, tiled=True)  9.49 us
    all_to_all x1, starting transfers between devices, shards(): lax.all_to_all(outgoing, 'group', split_axis=0, concat_axis=0, tiled=True)  9.3 us
    all_to_all x1, waiting for transfers between devices, shards(): lax.all_to_all(spread[source], 'group', 0, 0, tiled=True)  8.39 us
    all_to_all x1, waiting for transfers between devices, shards(): spread = lax.all_to_all(share[:, None, :], 'group', 0, 0, tiled=True)  8.02 us
    pallas_call x1, Pallas kernels, make_queries(): pl.pallas_call(query_kernel, grid=(heads // 2,), in_specs=[pl.BlockSpec((...  4.32 us
  transfers between devices with their start and end apart: 17, of which 3 were waited for; matrix products, arithmetic and copies ran while one was open for 10% of the time, Pallas kernels for 24%

profile of v1, /device:TPU:1, one launch (start us, length us, event | category | flops | bytes accessed | tf_op | source)
XLA Modules:
  0.0 137.0 jit_solution(9473733976064127410)
XLA Ops:
  0.7 1.2 copy-done
  1.9 2.3 %convolution_convert_fusion.a_ref = bf16[256,576]{1,0:T(8,128)(2,1)} fusion(bf16[256,896]{1,0:T(8,128)(2,1)} %param.11, bf16[896,576]{0,1:T(8,128)(2,1)S(1)} %copy-done), kind=kOutput, calls=%fused_computation.2 | convolution fusion | flops 264388608 | bytes 1785856 | tf_op jit(solution)/shard_map/dot_general | solution.py:295
  4.2 3.2 %collective-permute-start.7 = (bf16[256,576]{1,0:T(8,128)(2,1)}, bf16[256,576]{1,0:T(8,128)(2,1)}, u32[]{:S(2)}, u32[]{:S(2)}) collective-permute-start(bf16[256,576]{1,0:T(8,128)(2,1)} %convolution_convert_fusion.a_ref), channel_id=1, source_target_pairs={{0,1},{1,0},{2,3},{3,2},{4,5},{5,4},{6,7},{7,6},{8,9},{9,8},{10,11... | collective-permute-start | bytes 884744 | tf_op jit(solution)/shard_map/ppermute | solution.py:263
  8.2 0.8 select_reduce_fusion.2
  9.3 1.6 %copy.43 = bf16[128,4,576]{2,1,0:T(4,128)(2,1)S(1)} copy(bf16[128,4,576]{0,2,1:T(8,128)(2,1)} %param.18) | data formatting | bytes 1179648 | tf_op args[7]
  10.8 1.6 %gather_fusion = bf16[64,4,576]{2,1,0:T(4,128)(2,1)} fusion(bf16[128,4,576]{2,1,0:T(4,128)(2,1)S(1)} %copy.43, s32[1024]{0:T(1024)S(1)} %pad_clamp_fusion.1), kind=kCustom, calls=%fused_computation | custom fusion | bytes 590080 | tf_op jit(solution)/shard_map/gather | solution.py:277
  12.4 9.3 %all-to-all-start = ((bf16[32,2,4,576]{3,2,1,0:T(4,128)(2,1)}), bf16[32,2,4,576]{3,2,1,0:T(4,128)(2,1)S(1)}, u32[]{:S(2)}, u32[]{:S(2)}) async-start(bf16[32,2,4,576]{3,2,1,0:T(4,128)(2,1)} %bitcast.40), calls=%async_computation | async-start | bytes 655360 | tf_op jit(solution)/shard_map/all_to_all | solution.py:278
  29.9 2.3 %copy-done.3 = bf16[1536,1536]{1,0:T(8,128)(2,1)S(1)} copy-done((bf16[1536,1536]{1,0:T(8,128)(2,1)S(1)}, bf16[1536,1536]{1,0:T(8,128)(2,1)}, u32[]{:S(2)}) %copy-start.3) | copy-done | bytes 4718616
  32.2 4.3 %queries.1.refs_2_ = bf16[8,640,256]{2,1,0:T(8,128)(2,1)S(1)} custom-call(bf16[256,1536]{1,0:T(8,128)(2,1)S(1)} %copy-done.6, bf16[1536,1536]{1,0:T(8,128)(2,1)S(1)} %copy-done.3, bf16[512,1024]{1,0:T(8,128)(2,1)S(1)} %copy-done.4, f32[32,256]{1,0:T(8,128)S(1)} %get-tuple-element.29.cos_ref, f32[32,256]{1,0:T(8,128)S(1)} %get-tuple-element.28.sin_ref), custom_call_target="tpu_custom_call" | custom-call | flops 1476395008 | bytes 8388608 | tf_op jit(solution)/shard_map/queries/pallas_call | solution.py:64
  36.5 1.5 %copy-done.1 = bf16[8,640,256]{2,1,0:T(8,128)(2,1)} copy-done((bf16[8,640,256]{2,1,0:T(8,128)(2,1)}, bf16[8,640,256]{2,1,0:T(8,128)(2,1)S(1)}, u32[]{:S(2)}) %copy-start.1) | copy-done | bytes 2621464
  38.0 0.8 multiply_sine_fusion
  38.8 1.9 %combine.1 = (f32[64,576]{1,0:T(8,128)}, bf16[64,576]{1,0:T(8,128)(2,1)}, bf16[64,576]{1,0:T(8,128)(2,1)}, bf16[64,576]{1,0:T(8,128)(2,1)}) custom-call(s32[1]{0:T(128)} %bitcast.19.y_ref, bf16[256,576]{1,0:T(8,128)(2,1)} %convolution_convert_fusion.a_ref, bf16[256,576]{1,0:T(8,128)(2,1)} %collective-permute-done.7.b_ref), custom_call_target="tpu_custom_call" | custom-call | flops 147456 | bytes 1179648 | tf_op jit(solution)/shard_map/combine/pallas_call | solution.py:99
  40.7 2.9 %collective-permute-start.10 = (bf16[64,576]{1,0:T(8,128)(2,1)}, bf16[64,576]{1,0:T(8,128)(2,1)S(1)}, u32[]{:S(2)}, u32[]{:S(2)}) collective-permute-start(bf16[64,576]{1,0:T(8,128)(2,1)} %get-tuple-element.15), channel_id=1, source_target_pairs={{0,4},{1,5},{2,6},{3,7},{4,0},{5,1},{6,2},{7,3},{8,12},{9,13},{10,... | collective-permute-start | bytes 221192 | tf_op jit(solution)/shard_map/ppermute | solution.py:263
  44.0 2.3 %collective-permute-start.9 = (bf16[64,576]{1,0:T(8,128)(2,1)}, bf16[64,576]{1,0:T(8,128)(2,1)S(1)}, u32[]{:S(2)}, u32[]{:S(2)}) collective-permute-start(bf16[64,576]{1,0:T(8,128)(2,1)} %get-tuple-element.14), channel_id=1, source_target_pairs={{0,6},{1,7},{2,0},{3,1},{4,2},{5,3},{6,4},{7,5},{8,14},{9,15},{10,... | collective-permute-start | bytes 221192 | tf_op jit(solution)/shard_map/ppermute | solution.py:263
  46.3 2.0 %collective-permute-done.8.a_ref = bf16[64,576]{1,0:T(8,128)(2,1)S(1)} collective-permute-done((bf16[64,576]{1,0:T(8,128)(2,1)}, bf16[64,576]{1,0:T(8,128)(2,1)S(1)}, u32[]{:S(2)}, u32[]{:S(2)}) %collective-permute-start.8) | collective-permute-done | bytes 73760 | tf_op jit(solution)/shard_map/ppermute | solution.py:263
  49.0 1.8 %finish.1.refs_5_ = bf16[64,576]{1,0:T(8,128)(2,1)} custom-call(f32[64,576]{1,0:T(8,128)} %get-tuple-element.12.own_ref, bf16[64,576]{1,0:T(8,128)(2,1)} %copy-done.9, bf16[64,576]{1,0:T(8,128)(2,1)} %copy-done.10, bf16[64,576]{1,0:T(8,128)(2,1)} %copy-done.8, f32[1,512]{1,0:T(1,128)} %bitcast.43, f32[64,32]{1,0:T(8,128)} %get-tuple-element.31.cos_ref, ...), custom_call_target="tpu_custom_call" | custom-call | flops 294912 | bytes 442368 | tf_op jit(solution)/shard_map/finish/pallas_call | solution.py:123
  50.9 1.5 %collective-permute-start.11 = (bf16[64,576]{1,0:T(8,128)(2,1)}, bf16[64,576]{1,0:T(8,128)(2,1)S(1)}, u32[]{:S(2)}, u32[]{:S(2)}) collective-permute-start(bf16[64,576]{1,0:T(8,128)(2,1)} %finish.1.refs_5_), channel_id=1, source_target_pairs={{0,2},{1,3},{2,4},{3,5},{4,6},{5,7},{6,0},{7,1},{8,10},{9,11},{10,... | collective-permute-start | bytes 221192 | tf_op jit(solution)/shard_map/ppermute | solution.py:263
  52.5 1.1 collective-permute-start.6
  53.9 2.3 %collective-permute-start.4 = (bf16[256,576]{1,0:T(8,128)(2,1)S(1)}, bf16[256,576]{1,0:T(8,128)(2,1)}, u32[]{:S(2)}, u32[]{:S(2)}) collective-permute-start(bf16[256,576]{1,0:T(8,128)(2,1)S(1)} %reshape.208.refs_3_), channel_id=1, source_target_pairs={{0,6},{1,7},{2,0},{3,1},{4,2},{5,3},{6,4},{7,5},{8,14},{9,15},{10,... | collective-permute-start | bytes 884744 | tf_op jit(solution)/shard_map/ppermute | solution.py:263
  56.2 2.4 %collective-permute-start = (bf16[256,576]{1,0:T(8,128)(2,1)S(1)}, bf16[256,576]{1,0:T(8,128)(2,1)S(1)}, u32[]{:S(2)}, u32[]{:S(2)}) collective-permute-start(bf16[256,576]{1,0:T(8,128)(2,1)S(1)} %reshape.208.refs_3_), channel_id=1, source_target_pairs={{0,4},{1,5},{2,6},{3,7},{4,0},{5,1},{6,2},{7,3},{8,12},{9,13},{10,... | collective-permute-start | bytes 884744 | tf_op jit(solution)/shard_map/ppermute | solution.py:263
  58.7 0.8 dynamic-slice_bitcast_fusion
  60.6 0.7 reshape.229
  61.4 9.5 %all-to-all-start.1 = ((bf16[32,2,288]{2,1,0:T(2,128)(2,1)}), bf16[32,2,288]{2,1,0:T(2,128)(2,1)S(1)}, u32[]{:S(2)}, u32[]{:S(2)}) async-start(bf16[32,2,288]{2,1,0:T(2,128)(2,1)} %reshape.229), calls=%async_computation.1 | async-start | bytes 98304 | tf_op jit(solution)/shard_map/all_to_all | solution.py:307
  71.7 8.0 %all-to-all-done.1 = bf16[32,2,288]{2,1,0:T(2,128)(2,1)S(1)} async-done(((bf16[32,2,288]{2,1,0:T(2,128)(2,1)}), bf16[32,2,288]{2,1,0:T(2,128)(2,1)S(1)}, u32[]{:S(2)}, u32[]{:S(2)}) %all-to-all-start.1) | async-done | bytes 36896 | tf_op jit(solution)/shard_map/all_to_all | solution.py:307
  81.8 4.0 %all-to-all-start.2 = ((bf16[32,2,288]{2,1,0:T(2,128)(2,1)}), bf16[32,2,288]{2,1,0:T(2,128)(2,1)S(1)}, u32[]{:S(2)}, u32[]{:S(2)}) async-start(bf16[32,2,288]{2,1,0:T(2,128)(2,1)} %reshape.231), calls=%async_computation.2 | async-start | bytes 98304 | tf_op jit(solution)/shard_map/all_to_all | solution.py:309
  86.3 8.4 %all-to-all-done.2 = bf16[32,2,288]{2,1,0:T(2,128)(2,1)S(1)} async-done(((bf16[32,2,288]{2,1,0:T(2,128)(2,1)}), bf16[32,2,288]{2,1,0:T(2,128)(2,1)S(1)}, u32[]{:S(2)}, u32[]{:S(2)}) %all-to-all-start.2) | async-done | bytes 36896 | tf_op jit(solution)/shard_map/all_to_all | solution.py:309
  95.4 3.4 %collective-permute-start.3 = (bf16[256,576]{1,0:T(8,128)(2,1)S(1)}, bf16[256,576]{1,0:T(8,128)(2,1)S(1)}, u32[]{:S(2)}, u32[]{:S(2)}) collective-permute-start(bf16[256,576]{1,0:T(8,128)(2,1)S(1)} %collective-permute-done.2.refs_3_), channel_id=1, source_target_pairs={{0,1},{1,0},{2,3},{3,2},{4,5},{5,4},{6,7},{7,6},{8,9},{9,8},{10,11... | collective-permute-start | bytes 884744 | tf_op jit(solution)/shard_map/ppermute | solution.py:263
  99.4 1.7 %copy-done.2 = bf16[8,640,256]{2,1,0:T(8,128)(2,1)S(1)} copy-done((bf16[8,640,256]{2,1,0:T(8,128)(2,1)S(1)}, bf16[8,640,256]{2,1,0:T(8,128)(2,1)}, u32[]{:S(2)}) %copy-start.2) | copy-done | bytes 2621464
  101.1 0.9 copy-done.7
  102.0 10.7 %attention.3 = (f32[8,256]{1,0:T(8,128)S(1)}, f32[8,256]{1,0:T(8,128)S(1)}, f32[8,512,256]{2,1,0:T(8,128)S(1)}) custom-call(s32[6]{0:T(128)S(1)} %stack.83.refs_0_, s32[256,1]{1,0:T(8,128)S(1)} %add.177.refs_1_, bf16[8,640,256]{2,1,0:T(8,128)(2,1)S(1)} %copy-done.2, bf16[256,576]{1,0:T(8,128)(2,1)S(1)} %reshape.208.refs_3_, ...), custom_call_target="tpu_custom_call" | custom-call | flops 3623878656 | bytes 8388608 | tf_op jit(solution)/shard_map/attention/pallas_call | solution.py:224
  112.7 14.3 %attention.4 = (f32[8,256]{1,0:T(8,128)S(1)}, f32[8,256]{1,0:T(8,128)S(1)}, f32[8,512,256]{2,1,0:T(8,128)S(1)}) custom-call(s32[4]{0:T(128)S(1)} %pad_add_fusion.1.refs_0_, s32[256,1]{1,0:T(8,128)S(1)} %add.177.refs_1_, bf16[8,640,256]{2,1,0:T(8,128)(2,1)S(1)} %copy-done.2, bf16[256,576]{1,0:T(8,128)(2,1)S(1)} %collective-permute-done.2.refs_3_, ...), custom_call_target="tpu_custom_call" | custom-call | flops 4831838208 | bytes 8388608 | tf_op jit(solution)/shard_map/attention/pallas_call | solution.py:224
  127.1 10.0 %attention.5 = bf16[256,1024]{1,0:T(8,128)(2,1)} custom-call(s32[2]{0:T(128)S(1)} %pad_add_fusion.refs_0_, s32[256,1]{1,0:T(8,128)S(1)} %add.177.refs_1_, bf16[8,640,256]{2,1,0:T(8,128)(2,1)S(1)} %copy-done.2, bf16[256,576]{1,0:T(8,128)(2,1)S(1)} %collective-permute-done.refs_3_, bf16[256,576]{1,0:T(8,128)(2,1)S(1)} %collective-permute-done.1.refs_4_, ...), custom_call_target="tpu_custom_call" | custom-call | flops 2415919104 | bytes 8388608 | tf_op jit(solution)/shard_map/attention/pallas_call | solution.py:224
  (74 shorter events, 10.5 us)
Async XLA Ops:
  0.6 1.2 copy-start
  0.6 21.2 %copy-start.11 = (s32[32]{0:T(128)S(1)}, s32[32]{0:T(128)}, u32[]{:S(2)}) copy-start(s32[32]{0:T(128)} %param.20) | copy-start | bytes 388
  0.7 28.8 %copy-start.12 = (s32[32]{0:T(128)S(1)}, s32[32]{0:T(128)}, u32[]{:S(2)}) copy-start(s32[32]{0:T(128)} %param.21) | copy-start | bytes 388
  0.7 29.2 %copy-start.6 = (bf16[256,1536]{1,0:T(8,128)(2,1)S(1)}, bf16[256,1536]{1,0:T(8,128)(2,1)}, u32[]{:S(2)}) copy-start(bf16[256,1536]{1,0:T(8,128)(2,1)} %ql_ref.1) | copy-start | bytes 2359300
  0.7 29.2 %copy-start.4 = (bf16[512,1024]{1,0:T(8,128)(2,1)S(1)}, bf16[512,1024]{1,0:T(8,128)(2,1)}, u32[]{:S(2)}) copy-start(bf16[512,1024]{1,0:T(8,128)(2,1)} %wk_ref.1) | copy-start | bytes 3145732
  4.2 34.6 %collective-permute-start.7 = (bf16[256,576]{1,0:T(8,128)(2,1)}, bf16[256,576]{1,0:T(8,128)(2,1)}, u32[]{:S(2)}, u32[]{:S(2)}) collective-permute-start(bf16[256,576]{1,0:T(8,128)(2,1)} %convolution_convert_fusion.a_ref), channel_id=1, source_target_pairs={{0,1},{1,0},{2,3},{3,2},{4,5},{5,4},{6,7},{7,6},{8,9},{9,8},{10,11... | collective-permute-start | bytes 884744 | tf_op jit(solution)/shard_map/ppermute | solution.py:263
  12.4 39.9 %all-to-all-start = ((bf16[32,2,4,576]{3,2,1,0:T(4,128)(2,1)}), bf16[32,2,4,576]{3,2,1,0:T(4,128)(2,1)S(1)}, u32[]{:S(2)}, u32[]{:S(2)}) async-start(bf16[32,2,4,576]{3,2,1,0:T(4,128)(2,1)} %bitcast.40), calls=%async_computation | async-start | bytes 655360 | tf_op jit(solution)/shard_map/all_to_all | solution.py:278
  29.9 2.3 %copy-start.3 = (bf16[1536,1536]{1,0:T(8,128)(2,1)S(1)}, bf16[1536,1536]{1,0:T(8,128)(2,1)}, u32[]{:S(2)}) copy-start(bf16[1536,1536]{1,0:T(8,128)(2,1)} %wq_ref.1) | copy-start | bytes 14155780
  36.5 1.5 %copy-start.1 = (bf16[8,640,256]{2,1,0:T(8,128)(2,1)}, bf16[8,640,256]{2,1,0:T(8,128)(2,1)S(1)}, u32[]{:S(2)}) copy-start(bf16[8,640,256]{2,1,0:T(8,128)(2,1)S(1)} %queries.1.refs_2_) | copy-start | bytes 7864324
  40.7 5.6 %collective-permute-start.10 = (bf16[64,576]{1,0:T(8,128)(2,1)}, bf16[64,576]{1,0:T(8,128)(2,1)S(1)}, u32[]{:S(2)}, u32[]{:S(2)}) collective-permute-start(bf16[64,576]{1,0:T(8,128)(2,1)} %get-tuple-element.15), channel_id=1, source_target_pairs={{0,4},{1,5},{2,6},{3,7},{4,0},{5,1},{6,2},{7,3},{8,12},{9,13},{10,... | collective-permute-start | bytes 221192 | tf_op jit(solution)/shard_map/ppermute | solution.py:263
  43.6 4.7 %collective-permute-start.8 = (bf16[64,576]{1,0:T(8,128)(2,1)}, bf16[64,576]{1,0:T(8,128)(2,1)S(1)}, u32[]{:S(2)}, u32[]{:S(2)}) collective-permute-start(bf16[64,576]{1,0:T(8,128)(2,1)} %get-tuple-element.13), channel_id=1, source_target_pairs={{0,2},{1,3},{2,4},{3,5},{4,6},{5,7},{6,0},{7,1},{8,10},{9,11},{10,... | collective-permute-start | bytes 221192 | tf_op jit(solution)/shard_map/ppermute | solution.py:263
  44.0 4.3 %collective-permute-start.9 = (bf16[64,576]{1,0:T(8,128)(2,1)}, bf16[64,576]{1,0:T(8,128)(2,1)S(1)}, u32[]{:S(2)}, u32[]{:S(2)}) collective-permute-start(bf16[64,576]{1,0:T(8,128)(2,1)} %get-tuple-element.14), channel_id=1, source_target_pairs={{0,6},{1,7},{2,0},{3,1},{4,2},{5,3},{6,4},{7,5},{8,14},{9,15},{10,... | collective-permute-start | bytes 221192 | tf_op jit(solution)/shard_map/ppermute | solution.py:263
  46.3 2.0 %copy-start.8 = (bf16[64,576]{1,0:T(8,128)(2,1)}, bf16[64,576]{1,0:T(8,128)(2,1)S(1)}, u32[]{:S(2)}) copy-start(bf16[64,576]{1,0:T(8,128)(2,1)S(1)} %collective-permute-done.10.c_ref) | copy-start | bytes 221188
  48.3 0.6 copy-start.9
  48.3 0.7 copy-start.10
  50.9 20.0 %collective-permute-start.11 = (bf16[64,576]{1,0:T(8,128)(2,1)}, bf16[64,576]{1,0:T(8,128)(2,1)S(1)}, u32[]{:S(2)}, u32[]{:S(2)}) collective-permute-start(bf16[64,576]{1,0:T(8,128)(2,1)} %finish.1.refs_5_), channel_id=1, source_target_pairs={{0,2},{1,3},{2,4},{3,5},{4,6},{5,7},{6,0},{7,1},{8,10},{9,11},{10,... | collective-permute-start | bytes 221192 | tf_op jit(solution)/shard_map/ppermute | solution.py:263
  52.5 46.9 %collective-permute-start.6 = (bf16[256,576]{1,0:T(8,128)(2,1)S(1)}, bf16[256,576]{1,0:T(8,128)(2,1)S(1)}, u32[]{:S(2)}, u32[]{:S(2)}) collective-permute-start(bf16[256,576]{1,0:T(8,128)(2,1)S(1)} %reshape.208.refs_3_), channel_id=1, source_target_pairs={{0,1},{1,0},{2,3},{3,2},{4,5},{5,4},{6,7},{7,6},{8,9},{9,8},{10,11... | collective-permute-start | bytes 884744 | tf_op jit(solution)/shard_map/ppermute | solution.py:263
  53.5 41.8 %collective-permute-start.2 = (bf16[256,576]{1,0:T(8,128)(2,1)S(1)}, bf16[256,576]{1,0:T(8,128)(2,1)S(1)}, u32[]{:S(2)}, u32[]{:S(2)}) collective-permute-start(bf16[256,576]{1,0:T(8,128)(2,1)S(1)} %reshape.208.refs_3_), channel_id=1, source_target_pairs={{0,2},{1,3},{2,4},{3,5},{4,6},{5,7},{6,0},{7,1},{8,10},{9,11},{10,... | collective-permute-start | bytes 884744 | tf_op jit(solution)/shard_map/ppermute | solution.py:263
  53.9 44.9 %collective-permute-start.4 = (bf16[256,576]{1,0:T(8,128)(2,1)S(1)}, bf16[256,576]{1,0:T(8,128)(2,1)}, u32[]{:S(2)}, u32[]{:S(2)}) collective-permute-start(bf16[256,576]{1,0:T(8,128)(2,1)S(1)} %reshape.208.refs_3_), channel_id=1, source_target_pairs={{0,6},{1,7},{2,0},{3,1},{4,2},{5,3},{6,4},{7,5},{8,14},{9,15},{10,... | collective-permute-start | bytes 884744 | tf_op jit(solution)/shard_map/ppermute | solution.py:263
  56.2 42.7 %collective-permute-start = (bf16[256,576]{1,0:T(8,128)(2,1)S(1)}, bf16[256,576]{1,0:T(8,128)(2,1)S(1)}, u32[]{:S(2)}, u32[]{:S(2)}) collective-permute-start(bf16[256,576]{1,0:T(8,128)(2,1)S(1)} %reshape.208.refs_3_), channel_id=1, source_target_pairs={{0,4},{1,5},{2,6},{3,7},{4,0},{5,1},{6,2},{7,3},{8,12},{9,13},{10,... | collective-permute-start | bytes 884744 | tf_op jit(solution)/shard_map/ppermute | solution.py:263
  61.4 18.3 %all-to-all-start.1 = ((bf16[32,2,288]{2,1,0:T(2,128)(2,1)}), bf16[32,2,288]{2,1,0:T(2,128)(2,1)S(1)}, u32[]{:S(2)}, u32[]{:S(2)}) async-start(bf16[32,2,288]{2,1,0:T(2,128)(2,1)} %reshape.229), calls=%async_computation.1 | async-start | bytes 98304 | tf_op jit(solution)/shard_map/all_to_all | solution.py:307
  70.9 15.0 %collective-permute-start.12 = (bf16[64,576]{1,0:T(8,128)(2,1)}, bf16[64,576]{1,0:T(8,128)(2,1)S(1)}, u32[]{:S(2)}, u32[]{:S(2)}) collective-permute-start(bf16[64,576]{1,0:T(8,128)(2,1)} %finish.1.refs_5_), channel_id=1, source_target_pairs={{0,6},{1,7},{2,0},{3,1},{4,2},{5,3},{6,4},{7,5},{8,14},{9,15},{10,... | collective-permute-start | bytes 221192 | tf_op jit(solution)/shard_map/ppermute | solution.py:263
  81.8 12.8 %all-to-all-start.2 = ((bf16[32,2,288]{2,1,0:T(2,128)(2,1)}), bf16[32,2,288]{2,1,0:T(2,128)(2,1)S(1)}, u32[]{:S(2)}, u32[]{:S(2)}) async-start(bf16[32,2,288]{2,1,0:T(2,128)(2,1)} %reshape.231), calls=%async_computation.2 | async-start | bytes 98304 | tf_op jit(solution)/shard_map/all_to_all | solution.py:309
  85.9 13.5 %collective-permute-start.13 = (bf16[64,576]{1,0:T(8,128)(2,1)}, bf16[64,576]{1,0:T(8,128)(2,1)S(1)}, u32[]{:S(2)}, u32[]{:S(2)}) collective-permute-start(bf16[64,576]{1,0:T(8,128)(2,1)} %finish.1.refs_5_), channel_id=1, source_target_pairs={{0,4},{1,5},{2,6},{3,7},{4,0},{5,1},{6,2},{7,3},{8,12},{9,13},{10,... | collective-permute-start | bytes 221192 | tf_op jit(solution)/shard_map/ppermute | solution.py:263
  95.4 17.3 %collective-permute-start.3 = (bf16[256,576]{1,0:T(8,128)(2,1)S(1)}, bf16[256,576]{1,0:T(8,128)(2,1)S(1)}, u32[]{:S(2)}, u32[]{:S(2)}) collective-permute-start(bf16[256,576]{1,0:T(8,128)(2,1)S(1)} %collective-permute-done.2.refs_3_), channel_id=1, source_target_pairs={{0,1},{1,0},{2,3},{3,2},{4,5},{5,4},{6,7},{7,6},{8,9},{9,8},{10,11... | collective-permute-start | bytes 884744 | tf_op jit(solution)/shard_map/ppermute | solution.py:263
  98.8 13.8 %collective-permute-start.5 = (bf16[256,576]{1,0:T(8,128)(2,1)}, bf16[256,576]{1,0:T(8,128)(2,1)S(1)}, u32[]{:S(2)}, u32[]{:S(2)}) collective-permute-start(bf16[256,576]{1,0:T(8,128)(2,1)} %collective-permute-done.4.refs_5_), channel_id=1, source_target_pairs={{0,1},{1,0},{2,3},{3,2},{4,5},{5,4},{6,7},{7,6},{8,9},{9,8},{10,11... | collective-permute-start | bytes 884744 | tf_op jit(solution)/shard_map/ppermute | solution.py:263
  98.9 28.1 %collective-permute-start.1 = (bf16[256,576]{1,0:T(8,128)(2,1)S(1)}, bf16[256,576]{1,0:T(8,128)(2,1)S(1)}, u32[]{:S(2)}, u32[]{:S(2)}) collective-permute-start(bf16[256,576]{1,0:T(8,128)(2,1)S(1)} %collective-permute-done.refs_3_), channel_id=1, source_target_pairs={{0,1},{1,0},{2,3},{3,2},{4,5},{5,4},{6,7},{7,6},{8,9},{9,8},{10,11... | collective-permute-start | bytes 884744 | tf_op jit(solution)/shard_map/ppermute | solution.py:263
  99.4 1.7 %copy-start.2 = (bf16[8,640,256]{2,1,0:T(8,128)(2,1)S(1)}, bf16[8,640,256]{2,1,0:T(8,128)(2,1)}, u32[]{:S(2)}) copy-start(bf16[8,640,256]{2,1,0:T(8,128)(2,1)} %copy-done.1) | copy-start | bytes 7864324
  101.1 0.9 copy-start.7
  112.7 14.4 %copy-start.5 = (bf16[512,1024]{1,0:T(8,128)(2,1)S(1)}, bf16[512,1024]{1,0:T(8,128)(2,1)}, u32[]{:S(2)}) copy-start(bf16[512,1024]{1,0:T(8,128)(2,1)} %refs_8_.1) | copy-start | bytes 3145732

commit v2 on v0

v2 whole, which is shorter than its diff:
```python
import functools

import jax
import jax.numpy as jnp
from jax import lax
from jax.experimental import pallas as pl
from jax.experimental.pallas import tpu as pltpu
from jax.sharding import PartitionSpec as P

NOPE = 128
ROPE = 64
VDIM = 128
KVR = 512
CAP = 2
LAT = KVR + ROPE
QWIDE = 256
HALF = ROPE // 2

rope_base = 50000.0
masked_value = -1e30
softmax_scale = float(NOPE + ROPE) ** (-0.5)
log2_scale = softmax_scale * 1.4426950408889634

MIB = 1 << 20
bf16 = jnp.bfloat16
f32 = jnp.float32


def vmem():
    return pl.BlockSpec(memory_space=pltpu.VMEM)


def hbm():
    return pl.BlockSpec(memory_space=pltpu.HBM)


def anywhere():
    return pl.BlockSpec(memory_space=pl.ANY)


def smem():
    return pl.BlockSpec(memory_space=pltpu.SMEM)


def select_kernel(table_ref, pool_ref, out_ref, pos_ref):
    group = lax.axis_index("group")
    page_rows, _, slot_count = pool_ref.shape
    requests, max_pages = table_ref.shape
    shift = slot_count.bit_length() - 1
    rows = requests * CAP * page_rows
    table = table_ref[...]
    page = lax.broadcasted_iota(jnp.int32, table.shape, 1)
    code = page * slot_count + (table & (slot_count - 1))
    mine = (table >> shift) == group
    first = jnp.min(jnp.where(mine, code, max_pages * slot_count), axis=1, keepdims=True) & (slot_count - 1)
    last = jnp.max(jnp.where(mine, code, 0), axis=1, keepdims=True) & (slot_count - 1)
    shape = (requests, CAP * page_rows, slot_count)
    part = lax.broadcasted_iota(jnp.int32, shape, 1)
    slot = lax.broadcasted_iota(jnp.int32, shape, 2)
    first = jnp.broadcast_to(first[:, :, None], shape)
    last = jnp.broadcast_to(last[:, :, None], shape)
    hit = slot == jnp.where(part < page_rows, first, last)
    total = None
    for u in range(page_rows):
        pick = jnp.where(jnp.logical_and(hit, part % page_rows == u), 1.0, 0.0).reshape(rows, slot_count).astype(bf16)
        term = lax.dot_general(pick, pool_ref[u], (((1,), (1,)), ((), ())), preferred_element_type=f32)
        total = term if total is None else total + term
    out_ref[...] = total.astype(bf16)
    owners = table_ref[pl.ds(group, 1), :] >> shift
    row = lax.broadcasted_iota(jnp.int32, (rows, max_pages), 0)
    column = lax.broadcasted_iota(jnp.int32, (rows, max_pages), 1)
    held = owners == row // (CAP * page_rows)
    first_page = jnp.min(jnp.where(held, column, max_pages), axis=1, keepdims=True)
    last_page = jnp.max(jnp.where(held, column, 0), axis=1, keepdims=True)
    one_row = lax.broadcasted_iota(jnp.int32, (rows, 1), 0)
    at = jnp.where((one_row // page_rows) % CAP == 0, first_page, last_page)
    pos_ref[...] = at * (page_rows * 8) + one_row % page_rows


def select(page_table, pool):
    rows = page_table.shape[0] * CAP * pool.shape[1]
    return pl.pallas_call(
        select_kernel,
        in_specs=[vmem(), vmem()],
        out_specs=[vmem(), vmem()],
        out_shape=[jax.ShapeDtypeStruct((rows, LAT), bf16), jax.ShapeDtypeStruct((rows, 1), jnp.int32)],
        cost_estimate=pl.CostEstimate(flops=8 * rows * 128 * LAT, bytes_accessed=1000000, transcendentals=0),
        name="select",
    )(page_table, jnp.transpose(pool, (1, 2, 0)))


def project_kernel(x_ref, w_ref, out_ref):
    total = lax.dot_general(x_ref[...], w_ref[...], (((1,), (1,)), ((), ())), preferred_element_type=f32)
    out_ref[...] = total.astype(bf16)


def project(x, w):
    return pl.pallas_call(
        project_kernel,
        in_specs=[vmem(), vmem()],
        out_specs=vmem(),
        out_shape=jax.ShapeDtypeStruct((x.shape[0], w.shape[0]), bf16),
        cost_estimate=pl.CostEstimate(flops=2 * x.size * w.shape[0], bytes_accessed=2 * (x.size + w.size),
                                      transcendentals=0),
        name="project",
    )(x, w)


def rotary(frequency, length, first_token, tokens):
    token = first_token + lax.broadcasted_iota(jnp.int32, (HALF, tokens), 1)
    angles = frequency * (length + token).astype(f32)
    return jnp.cos(angles), jnp.sin(angles)


def query_kernel(length_ref, frequency_ref, ql_ref, wq_hbm, out_ref, wq_ref, sems):
    heads, _, tokens = out_ref.shape
    pair_width = 2 * (NOPE + ROPE)
    copies = []
    for pair in range(heads // 2):
        columns = pl.ds(pair * pair_width, pair_width)
        copy = pltpu.make_async_copy(wq_hbm.at[:, columns], wq_ref.at[pair], sems.at[pair])
        copy.start()
        copies.append(copy)
    cosine, sine = rotary(frequency_ref[...], length_ref[lax.axis_index("group")], 0, tokens)
    row = lax.broadcasted_iota(jnp.int32, (QWIDE - NOPE - ROPE, tokens), 0)
    tail = jnp.where(row == 0, 1.0, 0.0).astype(bf16)
    for pair in range(heads // 2):
        copies[pair].wait()
        qt = jnp.dot(ql_ref[...], wq_ref[pair], preferred_element_type=f32).T
        for i in range(2):
            h = 2 * pair + i
            base = i * (NOPE + ROPE)
            first = qt[base + NOPE:base + NOPE + HALF]
            second = qt[base + NOPE + HALF:base + NOPE + ROPE]
            out_ref[h, :NOPE, :] = qt[base:base + NOPE].astype(bf16)
            out_ref[h, NOPE:NOPE + HALF, :] = (first * cosine - second * sine).astype(bf16)
            out_ref[h, NOPE + HALF:NOPE + ROPE, :] = (second * cosine + first * sine).astype(bf16)
            out_ref[h, NOPE + ROPE:, :] = tail


def make_queries(prefix_len, frequency, q_latent, w_q_b):
    tokens, rank = q_latent.shape
    heads = w_q_b.shape[1] // (NOPE + ROPE)
    return pl.pallas_call(
        query_kernel,
        in_specs=[smem(), vmem(), vmem(), hbm()],
        out_specs=vmem(),
        out_shape=jax.ShapeDtypeStruct((heads, QWIDE, tokens), bf16),
        scratch_shapes=[
            pltpu.VMEM((heads // 2, rank, 2 * (NOPE + ROPE)), bf16),
            pltpu.SemaphoreType.DMA((heads // 2,)),
        ],
        compiler_params=pltpu.CompilerParams(vmem_limit_bytes=24 * MIB),
        cost_estimate=pl.CostEstimate(flops=2 * tokens * rank * heads * 192, bytes_accessed=6 * MIB, transcendentals=0),
        name="queries",
    )(prefix_len, frequency, q_latent, w_q_b)


def combine_kernel(a_ref, b_ref, own_ref, up_ref, down_ref, far_ref):
    y = lax.axis_index("tensor") // 2
    rows = own_ref.shape[0]

    def part(d):
        start = pl.multiple_of(lax.rem(y + d, 4) * rows, rows)
        return a_ref[pl.ds(start, rows), :].astype(f32) + b_ref[pl.ds(start, rows), :].astype(f32)

    own_ref[...] = part(0)
    up_ref[...] = part(1).astype(bf16)
    far_ref[...] = part(2).astype(bf16)
    down_ref[...] = part(3).astype(bf16)


def combine(a, b):
    rows = a.shape[0] // 4
    return pl.pallas_call(
        combine_kernel,
        in_specs=[vmem(), vmem()],
        out_specs=[vmem()] * 4,
        out_shape=[jax.ShapeDtypeStruct((rows, LAT), f32)] + [jax.ShapeDtypeStruct((rows, LAT), bf16)] * 3,
        cost_estimate=pl.CostEstimate(flops=a.size, bytes_accessed=8 * a.size, transcendentals=0),
        name="combine",
    )(a, b)


def finish_kernel(length_ref, frequency_ref, own_ref, a_ref, b_ref, c_ref, gain_ref, _, out_ref, share_ref):
    total = (own_ref[...] + a_ref[...].astype(f32)) + (b_ref[...].astype(f32) + c_ref[...].astype(f32))
    rows = total.shape[0]
    nope = total[:, :KVR]
    mean_square = jnp.mean(nope * nope, axis=-1, keepdims=True)
    turned = total[:, KVR:LAT].T
    first = turned[:HALF]
    second = turned[HALF:]
    tensor = lax.axis_index("tensor")
    length = length_ref[lax.axis_index("group")]
    cosine, sine = rotary(frequency_ref[...], length, tensor // 2 * rows, rows)
    rotated = jnp.concatenate([first * cosine - second * sine, second * cosine + first * sine], axis=0).T
    out_ref[:, :KVR] = (nope * lax.rsqrt(mean_square + 1e-06) * gain_ref[...]).astype(bf16)
    out_ref[:, KVR:LAT] = rotated.astype(bf16)
    half = rows // 2
    core = lax.rem(tensor, 2)
    share_ref[...] = out_ref[pl.ds(pl.multiple_of(core * half, half), half), :]


def finish(prefix_len, frequency, own, a, b, c, gain, earlier):
    rows = own.shape[0]
    return pl.pallas_call(
        finish_kernel,
        in_specs=[smem()] + [vmem()] * 6 + [anywhere()],
        out_specs=[vmem(), vmem()],
        out_shape=[jax.ShapeDtypeStruct(own.shape, bf16), jax.ShapeDtypeStruct((rows // 2, LAT), bf16)],
        cost_estimate=pl.CostEstimate(flops=8 * own.size, bytes_accessed=12 * own.size, transcendentals=0),
        name="finish",
    )(prefix_len, frequency, own, a, b, c, gain, earlier)


def address_kernel(owner_ref, *refs):
    in_refs, out_ref = refs[:4], refs[4]
    group = lax.axis_index("group")
    x = lax.rem(group, 4)
    out_ref[...] = jnp.zeros_like(out_ref)
    for turn in range(4):
        owner = owner_ref[group - x + lax.rem(x - turn + 4, 4)]

        @pl.when(lax.rem(owner, 4) == x)
        def _():
            out_ref[owner // 4] = in_refs[turn][...]


def address(decode_owner, shares):
    rows = shares[0].shape[0]
    return pl.pallas_call(
        address_kernel,
        in_specs=[smem()] + [vmem()] * 4,
        out_specs=vmem(),
        out_shape=jax.ShapeDtypeStruct((8, rows, LAT), bf16),
        cost_estimate=pl.CostEstimate(flops=1000, bytes_accessed=20 * rows * LAT, transcendentals=0),
        name="address",
    )(decode_owner, *shares)


def pick_kernel(owner_ref, in_ref, _, out_ref, sem):
    group = lax.axis_index("group")
    request = jnp.int32(0)
    for r in range(owner_ref.shape[0]):
        request = request + jnp.where(owner_ref[r] == group, r, 0)
    copy = pltpu.make_async_copy(in_ref.at[request // 4], out_ref, sem)
    copy.start()
    copy.wait()


def pick(decode_owner, arrived, earlier):
    rows = arrived.shape[1]
    return pl.pallas_call(
        pick_kernel,
        in_specs=[smem(), anywhere(), anywhere()],
        out_specs=vmem(),
        out_shape=jax.ShapeDtypeStruct((rows, LAT), bf16),
        scratch_shapes=[pltpu.SemaphoreType.DMA],
        cost_estimate=pl.CostEstimate(flops=1000, bytes_accessed=4 * rows * LAT, transcendentals=0),
        name="pick",
    )(decode_owner, arrived, earlier)


def after(x, token):
    return pl.pallas_call(
        lambda x_ref, token_ref, out_ref: None,
        in_specs=[anywhere(), anywhere()],
        out_specs=anywhere(),
        out_shape=jax.ShapeDtypeStruct(x.shape, x.dtype),
        input_output_aliases={0: 0},
        cost_estimate=pl.CostEstimate(flops=0, bytes_accessed=0, transcendentals=0),
        name="after",
    )(x, token)


def attention_kernel(turns, length_ref, pos_ref, qt_ref, wk_hbm, wv_hbm, cached_ref, *refs):
    refs = list(refs)
    new_refs = [refs.pop(0) for _ in turns]
    out_ref, tails, keys, values, scores, weights, landed, fresh, wk_ref, wv_ref, sems, w_sems = refs
    heads, _, tokens = qt_ref.shape
    rows = pos_ref.shape[0]
    blocks = landed.shape[0]
    tiles = blocks + 1
    tensor = lax.axis_index("tensor")
    length = length_ref[lax.axis_index("group")]
    ups = []
    for pair in range(heads // 2):
        columns = pl.ds(pair * 256, 256)
        for i, (source, target) in enumerate(((wk_hbm, wk_ref), (wv_hbm, wv_ref))):
            copy = pltpu.make_async_copy(source.at[:, columns], target.at[:, columns], w_sems.at[2 * pair + i])
            copy.start()
            ups.append(copy)
    copies = []
    for b in range(blocks):
        copy = pltpu.make_async_copy(cached_ref.at[pl.ds(b * rows, rows), :], landed.at[b], sems.at[b])
        copy.start()
        copies.append(copy)
    latents = [landed.at[b] for b in range(blocks)] + [fresh]
    causal = []
    for b, turn in enumerate(turns):
        n = new_refs[b].shape[0]
        fresh[b * n:(b + 1) * n, :] = new_refs[b][...]
        key_token = lax.rem(tensor // 2 + turn, 4) * n + lax.broadcasted_iota(jnp.int32, (n, tokens), 0)
        causal.append(key_token <= lax.broadcasted_iota(jnp.int32, (n, tokens), 1))
    allowed = jnp.concatenate(causal, axis=0)
    lane = lax.broadcasted_iota(jnp.int32, (rows, 128 - ROPE), 1)

    def stage(j):
        here = slice(j * rows, (j + 1) * rows)
        if j < blocks:
            copies[j].wait()
            out_of_range = jnp.logical_and(pos_ref[...] >= length - 4 * j, lane == 0)
            tails[here, ROPE:] = jnp.where(out_of_range, masked_value, 0.0).astype(bf16)
        else:
            tails[here, ROPE:] = jnp.zeros((rows, 128 - ROPE), bf16)
        tails[here, :ROPE] = latents[j][:, KVR:LAT]

    def project_up(pair, j):
        here = slice(j * rows, (j + 1) * rows)
        nope = latents[j][:, :KVR]
        columns = slice(pair * 256, (pair + 1) * 256)
        k = jnp.dot(nope, wk_ref[:, columns], preferred_element_type=f32).astype(bf16)
        v = lax.dot_general(
            wv_ref[:, columns], nope, (((0,), (1,)), ((), ())), preferred_element_type=f32
        ).astype(bf16)
        for i in range(2):
            slot = 2 * (pair % 2) + i
            keys[slot, here, :NOPE] = k[:, i * NOPE:(i + 1) * NOPE]
            keys[slot, here, NOPE:] = tails[here, :]
            values[slot, :, here] = v[i * VDIM:(i + 1) * VDIM]

    def score(h, j):
        here = slice(j * rows, (j + 1) * rows)
        s = jnp.dot(keys[h % 4, here], qt_ref[h], preferred_element_type=f32)
        if j >= blocks:
            s = jnp.where(allowed, s, masked_value)
        scores[h % 2, here] = s
        return jnp.max(s, axis=0, keepdims=True)

    def weigh(h, j, top):
        here = slice(j * rows, (j + 1) * rows)
        p = jnp.exp2((scores[h % 2, here] - top) * log2_scale)
        weights[h % 2, here] = p.astype(bf16)
        return jnp.sum(p, axis=0, keepdims=True)

    order = [blocks] + list(range(blocks))
    tops = []
    for copy in ups[:2]:
        copy.wait()
    for j in order:
        stage(j)
        project_up(0, j)
        tops.append(score(0, j))
    for h in range(heads):
        top = functools.reduce(jnp.maximum, tops)
        tops = []
        norms = []
        if h % 2 == 0 and h + 2 < heads:
            for copy in ups[h + 2:h + 4]:
                copy.wait()
        for i, j in enumerate(order):
            if h // 2 * 2 + 2 < heads and i % 2 == h % 2:
                project_up(h // 2 + 1, j)
            if h + 1 < heads:
                tops.append(score(h + 1, j))
            norms.append(weigh(h, j, top))
        norm = functools.reduce(jnp.add, norms)
        acc = jnp.dot(values[h % 4], weights[h % 2], preferred_element_type=f32)
        out_ref[:, h * VDIM:(h + 1) * VDIM] = (acc / norm).T.astype(bf16)


def attention(prefix_len, pos, qt, w_key_up, w_value_up, cached, turns, new_blocks):
    heads, _, tokens = qt.shape
    rows = pos.shape[0]
    blocks = cached.shape[0] // rows
    total = rows * (blocks + 1)
    return pl.pallas_call(
        functools.partial(attention_kernel, turns),
        in_specs=[smem()] + [vmem()] * 2 + [hbm()] * 3 + [vmem()] * len(new_blocks),
        out_specs=vmem(),
        out_shape=jax.ShapeDtypeStruct((tokens, heads * VDIM), bf16),
        scratch_shapes=[
            pltpu.VMEM((total, 128), bf16),
            pltpu.VMEM((4, total, QWIDE), bf16),
            pltpu.VMEM((4, VDIM, total), bf16),
            pltpu.VMEM((2, total, tokens), f32),
            pltpu.VMEM((2, total, tokens), bf16),
            pltpu.VMEM((blocks, rows, LAT), bf16),
            pltpu.VMEM((rows, LAT), bf16),
            pltpu.VMEM(w_key_up.shape, bf16),
            pltpu.VMEM(w_value_up.shape, bf16),
            pltpu.SemaphoreType.DMA((blocks,)),
            pltpu.SemaphoreType.DMA((heads,)),
        ],
        compiler_params=pltpu.CompilerParams(vmem_limit_bytes=32 * MIB),
        cost_estimate=pl.CostEstimate(flops=4 * heads * tokens * total * 512, bytes_accessed=4 * MIB,
                                      transcendentals=heads * tokens * total),
        name="attention",
    )(prefix_len, pos, qt, w_key_up, w_value_up, cached, *new_blocks)


def shards(
    hidden,
    w_kv_a,
    kv_gain,
    q_latent,
    w_q_b,
    w_key_up,
    w_value_up,
    pool,
    page_table,
    prefix_len,
    decode_owner,
):

    def tensor_permute(x, step):
        return lax.ppermute(x, "tensor", [(i, step(i)) for i in range(8)])

    up = lambda i: (i + 2) % 8
    down = lambda i: (i - 2) % 8
    far = lambda i: (i + 4) % 8
    other = lambda i: i ^ 1

    outgoing, pos = select(page_table, pool)
    outgoing = outgoing.reshape(page_table.shape[0], -1, LAT)
    incoming = lax.all_to_all(outgoing, "group", split_axis=0, concat_axis=0, tiled=True)
    own_block = incoming.reshape(pos.shape[0], LAT)

    frequency = (rope_base ** (-2.0 * jnp.arange(HALF, dtype=f32) / ROPE))[:, None]
    qt = make_queries(prefix_len, frequency, q_latent, w_q_b)

    partial_sum = project(hidden, w_kv_a.T)
    partner_sum = tensor_permute(partial_sum, other)
    own, to_up, to_down, to_far = combine(partial_sum, partner_sum)
    from_down = tensor_permute(to_up, up)
    from_up = tensor_permute(to_down, down)
    from_far = tensor_permute(to_far, far)
    latent, share = finish(prefix_len, frequency, own, from_down, from_up, from_far, kv_gain[None, :], qt)
    latents = [latent, tensor_permute(latent, up), tensor_permute(latent, down), tensor_permute(latent, far)]

    def x_permute(turn):
        return lax.ppermute(share, "group", [(i, i // 4 * 4 + (i + turn) % 4) for i in range(32)])

    columns = [[4 * z + x for z in range(8)] for x in range(4)]
    addressed = address(decode_owner, [share, x_permute(1), x_permute(2), x_permute(3)])
    arrived = lax.all_to_all(addressed, "group", 0, 0, tiled=True, axis_index_groups=columns)

    own_block = after(own_block, own)
    cached = lax.all_gather(own_block, "tensor", axis=0, tiled=True)
    attn_out = attention(prefix_len, pos, qt, w_key_up, w_value_up, cached, (0, 3, 1, 2), latents)
    decode_pages = pick(decode_owner, arrived, attn_out)
    return (attn_out, decode_pages)


def solution(mesh):
    return jax.shard_map(
        shards,
        mesh=mesh,
        in_specs=(
            P("group", "tensor"),
            P("tensor", None),
            P(),
            P("group", None),
            P(None, "tensor"),
            P(None, "tensor"),
            P(None, "tensor"),
            P("group", "tensor", None),
            P(),
            P(),
            P(),
        ),
        out_specs=(P("group", "tensor"), P(("group", "tensor"), None)),
        check_vma=False,
    )
```

time: 241 us -> 99.7 us (0.41)
  the two profiles are of different devices: /device:TPU:1 before, /device:TPU:16 now
where the time goes in v2:
time: 99.7 us; the launch traced here: 99.1 us
  Pallas kernels  34.5 us (35%)
  starting transfers between devices  28.2 us (28%)
  between operations  14.3 us (14%)
  waiting for transfers between devices  11.5 us (12%)
  local copies, waits for them, and re-layouts  10.6 us (11%)
    pallas_call x1, Pallas kernels, attention(): pl.pallas_call(functools.partial(attention_kernel, turns), in_specs=[smem...  17.8 us
    all_to_all x1, starting transfers between devices, shards(): lax.all_to_all(outgoing, 'group', split_axis=0, concat_axis=0, tiled=True)  11.3 us
    unnamed x42, local copies, waits for them, and re-layouts  10.6 us
    ppermute x7, starting transfers between devices, tensor_permute(): return lax.ppermute(x, 'tensor', [(i, step(i)) for i in range(8)])  8.87 us
    all_to_all x1, waiting for transfers between devices, shards(): lax.all_to_all(outgoing, 'group', split_axis=0, concat_axis=0, tiled=True)  6.81 us
    ppermute x3, starting transfers between devices, x_permute(): lax.ppermute(share, 'group', [(i, i // 4 * 4 + (i + turn) % 4) for i in r...  4.55 us
    pallas_call x1, Pallas kernels, make_queries(): pl.pallas_call(query_kernel, in_specs=[smem(), vmem(), vmem(), hbm()], ou...  3.96 us
    all_to_all x1, starting transfers between devices, shards(): lax.all_to_all(addressed, 'group', 0, 0, tiled=True, axis_index_groups=co...  3.43 us
  transfers between devices with their start and end apart: 13, of which 4 were waited for; matrix products, arithmetic and copies ran while one was open for 0% of the time, Pallas kernels for 30%

profile of v2, /device:TPU:16, one launch (start us, length us, event | category | flops | bytes accessed | tf_op | source)
XLA Modules:
  0.0 99.1 jit_solution(18317400007655669040)
XLA Ops:
  7.2 2.5 %select.1 = (bf16[256,576]{1,0:T(8,128)(2,1)}, s32[256,1]{1,0:T(8,128)}) custom-call(s32[32,64]{1,0:T(8,128)} %table_ref.1, bf16[4,576,128]{2,1,0:T(8,128)(2,1)} %bitcast.7), custom_call_target="tpu_custom_call" | custom-call | flops 150994944 | bytes 1000000 | tf_op jit(solution)/shard_map/select/pallas_call | solution.py:82
  9.7 11.3 %all-to-all-start = ((bf16[32,8,576]{2,1,0:T(8,128)(2,1)}), bf16[32,8,576]{2,1,0:T(8,128)(2,1)S(1)}, u32[]{:S(2)}, u32[]{:S(2)}) async-start(bf16[32,8,576]{2,1,0:T(8,128)(2,1)} %bitcast.8), calls=%async_computation | async-start | bytes 655360 | tf_op jit(solution)/shard_map/all_to_all | solution.py:426
  21.1 2.7 %project.1.a_ref = bf16[256,576]{1,0:T(8,128)(2,1)} custom-call(bf16[256,896]{1,0:T(8,128)(2,1)} %x_ref.1, bf16[576,896]{1,0:T(8,128)(2,1)} %bitcast.6), custom_call_target="tpu_custom_call" | custom-call | flops 264241152 | bytes 1490944 | tf_op jit(solution)/shard_map/project/pallas_call | solution.py:98
  23.8 1.8 %collective-permute-done.b_ref = bf16[256,576]{1,0:T(8,128)(2,1)S(1)} collective-permute-done((bf16[256,576]{1,0:T(8,128)(2,1)}, bf16[256,576]{1,0:T(8,128)(2,1)S(1)}, u32[]{:S(2)}, u32[]{:S(2)}) %collective-permute-start) | collective-permute-done | bytes 294944 | tf_op jit(solution)/shard_map/ppermute | solution.py:417
  25.6 0.7 copy-done.14
  26.3 1.9 %combine.1 = (f32[64,576]{1,0:T(8,128)}, bf16[64,576]{1,0:T(8,128)(2,1)}, bf16[64,576]{1,0:T(8,128)(2,1)}, bf16[64,576]{1,0:T(8,128)(2,1)}) custom-call(bf16[256,576]{1,0:T(8,128)(2,1)} %project.1.a_ref, bf16[256,576]{1,0:T(8,128)(2,1)} %copy-done.14), custom_call_target="tpu_custom_call" | custom-call | flops 147456 | bytes 1179648 | tf_op jit(solution)/shard_map/combine/pallas_call | solution.py:175
  28.2 6.8 %all-to-all-done = bf16[32,8,576]{2,1,0:T(8,128)(2,1)S(1)} async-done(((bf16[32,8,576]{2,1,0:T(8,128)(2,1)}), bf16[32,8,576]{2,1,0:T(8,128)(2,1)S(1)}, u32[]{:S(2)}, u32[]{:S(2)}) %all-to-all-start) | async-done | bytes 294944 | tf_op jit(solution)/shard_map/all_to_all | solution.py:426
  35.0 0.7 copy-done.12
  35.8 1.4 %collective-permute-start.1 = (bf16[64,576]{1,0:T(8,128)(2,1)}, bf16[64,576]{1,0:T(8,128)(2,1)S(1)}, u32[]{:S(2)}, u32[]{:S(2)}) collective-permute-start(bf16[64,576]{1,0:T(8,128)(2,1)} %get-tuple-element.13), channel_id=1, source_target_pairs={{0,2},{1,3},{2,4},{3,5},{4,6},{5,7},{6,0},{7,1},{8,10},{9,11},{10,... | collective-permute-start | bytes 221192 | tf_op jit(solution)/shard_map/ppermute | solution.py:417
  37.2 0.7 collective-permute-start.2
  37.9 1.5 %collective-permute-start.3 = (bf16[64,576]{1,0:T(8,128)(2,1)}, bf16[64,576]{1,0:T(8,128)(2,1)S(1)}, u32[]{:S(2)}, u32[]{:S(2)}) collective-permute-start(bf16[64,576]{1,0:T(8,128)(2,1)} %get-tuple-element.15), channel_id=1, source_target_pairs={{0,4},{1,5},{2,6},{3,7},{4,0},{5,1},{6,2},{7,3},{8,12},{9,13},{10,... | collective-permute-start | bytes 221192 | tf_op jit(solution)/shard_map/ppermute | solution.py:417
  39.5 2.3 %copy-done = bf16[1536,1536]{1,0:T(8,128)(2,1)S(1)} copy-done((bf16[1536,1536]{1,0:T(8,128)(2,1)S(1)}, bf16[1536,1536]{1,0:T(8,128)(2,1)}, u32[]{:S(2)}) %copy-start) | copy-done | bytes 4718616
  41.8 4.0 %queries.1._.qt_ref = bf16[8,256,256]{2,1,0:T(8,128)(2,1)S(1)} custom-call(s32[32]{0:T(128)S(1)} %copy-done.5, f32[32,1]{1,0:T(8,128)S(1)} %multiply_power_fusion.frequency_ref, bf16[256,1536]{1,0:T(8,128)(2,1)S(1)} %copy-done.3, bf16[1536,1536]{1,0:T(8,128)(2,1)S(1)} %copy-done), custom_call_target="tpu_custom_call" | custom-call | flops 1207959552 | bytes 6291456 | tf_op jit(solution)/shard_map/queries/pallas_call | solution.py:144
  45.8 1.0 copy-done.1
  46.8 0.6 copy-done.15
  47.5 1.9 %finish.1 = (bf16[64,576]{1,0:T(8,128)(2,1)}, bf16[32,576]{1,0:T(8,128)(2,1)}) custom-call(s32[32]{0:T(128)} %length_ref.5, f32[32,1]{1,0:T(8,128)} %copy-done.4, f32[64,576]{1,0:T(8,128)} %get-tuple-element.12.token_ref.own_ref, bf16[64,576]{1,0:T(8,128)(2,1)} %copy-done.15, bf16[64,576]{1,0:T(8,128)(2,1)} %copy-done.16, bf16[64,576]{1,0:T(8,128)(2,1)} %copy-done.17, ...), custom_call_target="tpu_custom_call" | custom-call | flops 294912 | bytes 442368 | tf_op jit(solution)/shard_map/finish/pallas_call | solution.py:206
  49.8 1.0 collective-permute-start.4
  50.8 1.1 %collective-permute-start.5 = (bf16[64,576]{1,0:T(8,128)(2,1)}, bf16[64,576]{1,0:T(8,128)(2,1)S(1)}, u32[]{:S(2)}, u32[]{:S(2)}) collective-permute-start(bf16[64,576]{1,0:T(8,128)(2,1)} %get-tuple-element.16.refs_0_), channel_id=1, source_target_pairs={{0,6},{1,7},{2,0},{3,1},{4,2},{5,3},{6,4},{7,5},{8,14},{9,15},{10,... | collective-permute-start | bytes 221192 | tf_op jit(solution)/shard_map/ppermute | solution.py:417
  51.9 3.2 %collective-permute-start.6 = (bf16[64,576]{1,0:T(8,128)(2,1)}, bf16[64,576]{1,0:T(8,128)(2,1)S(1)}, u32[]{:S(2)}, u32[]{:S(2)}) collective-permute-start(bf16[64,576]{1,0:T(8,128)(2,1)} %get-tuple-element.16.refs_0_), channel_id=1, source_target_pairs={{0,4},{1,5},{2,6},{3,7},{4,0},{5,1},{6,2},{7,3},{8,12},{9,13},{10,... | collective-permute-start | bytes 221192 | tf_op jit(solution)/shard_map/ppermute | solution.py:417
  55.0 2.7 %collective-permute-start.8 = (bf16[32,576]{1,0:T(8,128)(2,1)}, bf16[32,576]{1,0:T(8,128)(2,1)S(1)}, u32[]{:S(2)}, u32[]{:S(2)}) collective-permute-start(bf16[32,576]{1,0:T(8,128)(2,1)} %get-tuple-element.17.refs_0_), channel_id=1, source_target_pairs={{0,16},{8,24},{16,0},{24,8},{32,48},{40,56},{48,32},{56,40},{64,80... | collective-permute-start | bytes 110600 | tf_op jit(solution)/shard_map/ppermute | solution.py:442
  57.7 1.5 %collective-permute-start.9 = (bf16[32,576]{1,0:T(8,128)(2,1)}, bf16[32,576]{1,0:T(8,128)(2,1)S(1)}, u32[]{:S(2)}, u32[]{:S(2)}) collective-permute-start(bf16[32,576]{1,0:T(8,128)(2,1)} %get-tuple-element.17.refs_0_), channel_id=1, source_target_pairs={{0,24},{8,0},{16,8},{24,16},{32,56},{40,32},{48,40},{56,48},{64,88... | collective-permute-start | bytes 110600 | tf_op jit(solution)/shard_map/ppermute | solution.py:442
  59.2 1.6 %collective-permute-done.8.refs_2_ = bf16[32,576]{1,0:T(8,128)(2,1)S(1)} collective-permute-done((bf16[32,576]{1,0:T(8,128)(2,1)}, bf16[32,576]{1,0:T(8,128)(2,1)S(1)}, u32[]{:S(2)}, u32[]{:S(2)}) %collective-permute-start.8) | collective-permute-done | bytes 36896 | tf_op jit(solution)/shard_map/ppermute | solution.py:442
  60.8 1.2 %collective-permute-done.9.refs_3_ = bf16[32,576]{1,0:T(8,128)(2,1)S(1)} collective-permute-done((bf16[32,576]{1,0:T(8,128)(2,1)}, bf16[32,576]{1,0:T(8,128)(2,1)S(1)}, u32[]{:S(2)}, u32[]{:S(2)}) %collective-permute-start.9) | collective-permute-done | bytes 36896 | tf_op jit(solution)/shard_map/ppermute | solution.py:442
  61.9 0.6 copy-done.20
  62.6 1.6 %address.1 = bf16[8,32,576]{2,1,0:T(8,128)(2,1)} custom-call(s32[32]{0:T(128)} %owner_ref.3, bf16[32,576]{1,0:T(8,128)(2,1)} %get-tuple-element.17.refs_0_, bf16[32,576]{1,0:T(8,128)(2,1)} %copy-done.18, bf16[32,576]{1,0:T(8,128)(2,1)} %copy-done.19, bf16[32,576]{1,0:T(8,128)(2,1)} %copy-done.20), custom_call_target="tpu_custom_call" | custom-call | flops 1000 | bytes 368640 | tf_op jit(solution)/shard_map/address/pallas_call | solution.py:231
  64.2 3.4 %all-to-all-start.1 = ((bf16[8,32,576]{2,1,0:T(8,128)(2,1)}), bf16[8,32,576]{2,1,0:T(8,128)(2,1)S(1)}, u32[]{:S(2)}, u32[]{:S(2)}) async-start(bf16[8,32,576]{2,1,0:T(8,128)(2,1)} %address.1), calls=%async_computation.1 | async-start | bytes 655360 | tf_op jit(solution)/shard_map/all_to_all | solution.py:446
  67.8 1.2 %copy-done.2 = bf16[8,256,256]{2,1,0:T(8,128)(2,1)S(1)} copy-done((bf16[8,256,256]{2,1,0:T(8,128)(2,1)S(1)}, bf16[8,256,256]{2,1,0:T(8,128)(2,1)}, u32[]{:S(2)}) %copy-start.2) | copy-done | bytes 1048600
  69.0 1.7 %copy-done.7 = bf16[2048,576]{1,0:T(8,128)(2,1)S(1)} copy-done((bf16[2048,576]{1,0:T(8,128)(2,1)S(1)}, bf16[2048,576]{1,0:T(8,128)(2,1)}, u32[]{:S(2)}) %copy-start.7) | copy-done | bytes 2359320
  70.7 0.9 copy-done.11
  71.6 17.8 %attention.1._ = bf16[256,1024]{1,0:T(8,128)(2,1)} custom-call(s32[32]{0:T(128)S(1)} %copy-done.6, s32[256,1]{1,0:T(8,128)S(1)} %copy-done.10, bf16[8,256,256]{2,1,0:T(8,128)(2,1)S(1)} %copy-done.2, bf16[512,1024]{1,0:T(8,128)(2,1)S(1)} %copy-done.8, bf16[512,1024]{1,0:T(8,128)(2,1)S(1)} %copy-done.9, bf16[2048,576]{1,0:T(8,128)(2,1)S(1)} %copy-done.7, ...), custom_call_target="tpu_custom_call" | custom-call | flops 9663676416 | bytes 4194304 | tf_op jit(solution)/shard_map/attention/pallas_call | solution.py:377
  89.4 0.7 copy-done.13
  90.1 2.1 %pick.1 = bf16[32,576]{1,0:T(8,128)(2,1)} custom-call(s32[32]{0:T(128)} %owner_ref.3, bf16[8,32,576]{2,1,0:T(8,128)(2,1)} %copy-done.13, bf16[256,1024]{1,0:T(8,128)(2,1)} %attention.1._), custom_call_target="tpu_custom_call" | custom-call | flops 1000 | bytes 73728 | tf_op jit(solution)/shard_map/pick/pallas_call | solution.py:253
  (47 shorter events, 0.7 us)
Async XLA Ops:
  7.2 32.3 %copy-start.5 = (s32[32]{0:T(128)S(1)}, s32[32]{0:T(128)}, u32[]{:S(2)}) copy-start(s32[32]{0:T(128)} %length_ref.5) | copy-start | bytes 388
  7.2 32.3 %copy-start.3 = (bf16[256,1536]{1,0:T(8,128)(2,1)S(1)}, bf16[256,1536]{1,0:T(8,128)(2,1)}, u32[]{:S(2)}) copy-start(bf16[256,1536]{1,0:T(8,128)(2,1)} %ql_ref.1) | copy-start | bytes 2359300
  9.7 25.3 %all-to-all-start = ((bf16[32,8,576]{2,1,0:T(8,128)(2,1)}), bf16[32,8,576]{2,1,0:T(8,128)(2,1)S(1)}, u32[]{:S(2)}, u32[]{:S(2)}) async-start(bf16[32,8,576]{2,1,0:T(8,128)(2,1)} %bitcast.8), calls=%async_computation | async-start | bytes 655360 | tf_op jit(solution)/shard_map/all_to_all | solution.py:426
  21.0 46.7 %all-gather.2.cloned.1.call-start = ((), (), s32[]{:S(2)}) async-start(), calls=%async_computation.2 | async-start | bytes 2949120 | tf_op jit(solution)/shard_map/all_gather | solution.py:449
  23.8 1.8 %collective-permute-start = (bf16[256,576]{1,0:T(8,128)(2,1)}, bf16[256,576]{1,0:T(8,128)(2,1)S(1)}, u32[]{:S(2)}, u32[]{:S(2)}) collective-permute-start(bf16[256,576]{1,0:T(8,128)(2,1)} %project.1.a_ref), channel_id=1, source_target_pairs={{0,1},{1,0},{2,3},{3,2},{4,5},{5,4},{6,7},{7,6},{8,9},{9,8},{10,11... | collective-permute-start | bytes 884744 | tf_op jit(solution)/shard_map/ppermute | solution.py:417
  25.6 0.7 copy-start.14
  26.3 41.4 %copy-start.10 = (s32[256,1]{1,0:T(8,128)S(1)}, s32[256,1]{1,0:T(8,128)}, u32[]{:S(2)}) copy-start(s32[256,1]{1,0:T(8,128)} %get-tuple-element.10.pos_ref) | copy-start | bytes 3076
  35.0 0.7 copy-start.12
  35.8 32.0 %copy-start.8 = (bf16[512,1024]{1,0:T(8,128)(2,1)S(1)}, bf16[512,1024]{1,0:T(8,128)(2,1)}, u32[]{:S(2)}) copy-start(bf16[512,1024]{1,0:T(8,128)(2,1)} %wk_hbm.1) | copy-start | bytes 3145732
  35.8 32.0 %copy-start.6 = (s32[32]{0:T(128)S(1)}, s32[32]{0:T(128)}, u32[]{:S(2)}) copy-start(s32[32]{0:T(128)} %length_ref.5) | copy-start | bytes 388
  35.8 11.0 %copy-start.4 = (f32[32,1]{1,0:T(8,128)}, f32[32,1]{1,0:T(8,128)S(1)}, u32[]{:S(2)}) copy-start(f32[32,1]{1,0:T(8,128)S(1)} %multiply_power_fusion.frequency_ref) | copy-start | bytes 388
  35.8 10.9 %collective-permute-start.1 = (bf16[64,576]{1,0:T(8,128)(2,1)}, bf16[64,576]{1,0:T(8,128)(2,1)S(1)}, u32[]{:S(2)}, u32[]{:S(2)}) collective-permute-start(bf16[64,576]{1,0:T(8,128)(2,1)} %get-tuple-element.13), channel_id=1, source_target_pairs={{0,2},{1,3},{2,4},{3,5},{4,6},{5,7},{6,0},{7,1},{8,10},{9,11},{10,... | collective-permute-start | bytes 221192 | tf_op jit(solution)/shard_map/ppermute | solution.py:417
  37.2 9.6 %collective-permute-start.2 = (bf16[64,576]{1,0:T(8,128)(2,1)}, bf16[64,576]{1,0:T(8,128)(2,1)S(1)}, u32[]{:S(2)}, u32[]{:S(2)}) collective-permute-start(bf16[64,576]{1,0:T(8,128)(2,1)} %get-tuple-element.14), channel_id=1, source_target_pairs={{0,6},{1,7},{2,0},{3,1},{4,2},{5,3},{6,4},{7,5},{8,14},{9,15},{10,... | collective-permute-start | bytes 221192 | tf_op jit(solution)/shard_map/ppermute | solution.py:417
  37.9 8.9 %collective-permute-start.3 = (bf16[64,576]{1,0:T(8,128)(2,1)}, bf16[64,576]{1,0:T(8,128)(2,1)S(1)}, u32[]{:S(2)}, u32[]{:S(2)}) collective-permute-start(bf16[64,576]{1,0:T(8,128)(2,1)} %get-tuple-element.15), channel_id=1, source_target_pairs={{0,4},{1,5},{2,6},{3,7},{4,0},{5,1},{6,2},{7,3},{8,12},{9,13},{10,... | collective-permute-start | bytes 221192 | tf_op jit(solution)/shard_map/ppermute | solution.py:417
  39.5 2.3 %copy-start = (bf16[1536,1536]{1,0:T(8,128)(2,1)S(1)}, bf16[1536,1536]{1,0:T(8,128)(2,1)}, u32[]{:S(2)}) copy-start(bf16[1536,1536]{1,0:T(8,128)(2,1)} %wq_hbm.1) | copy-start | bytes 14155780
  41.8 25.9 %copy-start.9 = (bf16[512,1024]{1,0:T(8,128)(2,1)S(1)}, bf16[512,1024]{1,0:T(8,128)(2,1)}, u32[]{:S(2)}) copy-start(bf16[512,1024]{1,0:T(8,128)(2,1)} %wv_hbm.1) | copy-start | bytes 3145732
  45.8 1.0 copy-start.1
  46.8 0.7 copy-start.16
  46.8 0.7 copy-start.17
  49.4 8.3 %collective-permute-start.7 = (bf16[32,576]{1,0:T(8,128)(2,1)}, bf16[32,576]{1,0:T(8,128)(2,1)S(1)}, u32[]{:S(2)}, u32[]{:S(2)}) collective-permute-start(bf16[32,576]{1,0:T(8,128)(2,1)} %get-tuple-element.17.refs_0_), channel_id=1, source_target_pairs={{0,8},{8,16},{16,24},{24,0},{32,40},{40,48},{48,56},{56,32},{64,72... | collective-permute-start | bytes 110600 | tf_op jit(solution)/shard_map/ppermute | solution.py:442
  49.8 17.8 %collective-permute-start.4 = (bf16[64,576]{1,0:T(8,128)(2,1)}, bf16[64,576]{1,0:T(8,128)(2,1)S(1)}, u32[]{:S(2)}, u32[]{:S(2)}) collective-permute-start(bf16[64,576]{1,0:T(8,128)(2,1)} %get-tuple-element.16.refs_0_), channel_id=1, source_target_pairs={{0,2},{1,3},{2,4},{3,5},{4,6},{5,7},{6,0},{7,1},{8,10},{9,11},{10,... | collective-permute-start | bytes 221192 | tf_op jit(solution)/shard_map/ppermute | solution.py:417
  50.8 16.9 %collective-permute-start.5 = (bf16[64,576]{1,0:T(8,128)(2,1)}, bf16[64,576]{1,0:T(8,128)(2,1)S(1)}, u32[]{:S(2)}, u32[]{:S(2)}) collective-permute-start(bf16[64,576]{1,0:T(8,128)(2,1)} %get-tuple-element.16.refs_0_), channel_id=1, source_target_pairs={{0,6},{1,7},{2,0},{3,1},{4,2},{5,3},{6,4},{7,5},{8,14},{9,15},{10,... | collective-permute-start | bytes 221192 | tf_op jit(solution)/shard_map/ppermute | solution.py:417
  51.9 15.8 %collective-permute-start.6 = (bf16[64,576]{1,0:T(8,128)(2,1)}, bf16[64,576]{1,0:T(8,128)(2,1)S(1)}, u32[]{:S(2)}, u32[]{:S(2)}) collective-permute-start(bf16[64,576]{1,0:T(8,128)(2,1)} %get-tuple-element.16.refs_0_), channel_id=1, source_target_pairs={{0,4},{1,5},{2,6},{3,7},{4,0},{5,1},{6,2},{7,3},{8,12},{9,13},{10,... | collective-permute-start | bytes 221192 | tf_op jit(solution)/shard_map/ppermute | solution.py:417
  55.0 5.7 %collective-permute-start.8 = (bf16[32,576]{1,0:T(8,128)(2,1)}, bf16[32,576]{1,0:T(8,128)(2,1)S(1)}, u32[]{:S(2)}, u32[]{:S(2)}) collective-permute-start(bf16[32,576]{1,0:T(8,128)(2,1)} %get-tuple-element.17.refs_0_), channel_id=1, source_target_pairs={{0,16},{8,24},{16,0},{24,8},{32,48},{40,56},{48,32},{56,40},{64,80... | collective-permute-start | bytes 110600 | tf_op jit(solution)/shard_map/ppermute | solution.py:442
  57.7 4.2 %copy-start.18 = (bf16[32,576]{1,0:T(8,128)(2,1)}, bf16[32,576]{1,0:T(8,128)(2,1)S(1)}, u32[]{:S(2)}) copy-start(bf16[32,576]{1,0:T(8,128)(2,1)S(1)} %collective-permute-done.7.refs_1_) | copy-start | bytes 110596
  57.7 4.2 %collective-permute-start.9 = (bf16[32,576]{1,0:T(8,128)(2,1)}, bf16[32,576]{1,0:T(8,128)(2,1)S(1)}, u32[]{:S(2)}, u32[]{:S(2)}) collective-permute-start(bf16[32,576]{1,0:T(8,128)(2,1)} %get-tuple-element.17.refs_0_), channel_id=1, source_target_pairs={{0,24},{8,0},{16,8},{24,16},{32,56},{40,32},{48,40},{56,48},{64,88... | collective-permute-start | bytes 110600 | tf_op jit(solution)/shard_map/ppermute | solution.py:442
  60.8 1.2 %copy-start.19 = (bf16[32,576]{1,0:T(8,128)(2,1)}, bf16[32,576]{1,0:T(8,128)(2,1)S(1)}, u32[]{:S(2)}) copy-start(bf16[32,576]{1,0:T(8,128)(2,1)S(1)} %collective-permute-done.8.refs_2_) | copy-start | bytes 110596
  64.2 25.2 %all-to-all-start.1 = ((bf16[8,32,576]{2,1,0:T(8,128)(2,1)}), bf16[8,32,576]{2,1,0:T(8,128)(2,1)S(1)}, u32[]{:S(2)}, u32[]{:S(2)}) async-start(bf16[8,32,576]{2,1,0:T(8,128)(2,1)} %address.1), calls=%async_computation.1 | async-start | bytes 655360 | tf_op jit(solution)/shard_map/all_to_all | solution.py:446
  67.8 1.2 %copy-start.2 = (bf16[8,256,256]{2,1,0:T(8,128)(2,1)S(1)}, bf16[8,256,256]{2,1,0:T(8,128)(2,1)}, u32[]{:S(2)}) copy-start(bf16[8,256,256]{2,1,0:T(8,128)(2,1)} %copy-done.1) | copy-start | bytes 3145732
  69.0 1.7 %copy-start.7 = (bf16[2048,576]{1,0:T(8,128)(2,1)S(1)}, bf16[2048,576]{1,0:T(8,128)(2,1)}, u32[]{:S(2)}) copy-start(bf16[2048,576]{1,0:T(8,128)(2,1)} %all-gather.2.cloned.1.call-done.cached_ref) | copy-start | bytes 7077892
  70.7 0.9 copy-start.11
  89.4 0.7 copy-start.13
  (2 other events, 1.2 us)
Sparse Core Ops, SparseCore 0:
  35.9 25.9 all-gather.1

commit v3 on v2

--- a/solution.py
+++ b/solution.py
@@ -2,6 +2,7 @@
 
 import jax
 import jax.numpy as jnp
+import numpy as np
 from jax import lax
 from jax.experimental import pallas as pl
 from jax.experimental.pallas import tpu as pltpu
@@ -14,6 +15,7 @@
 CAP = 2
 LAT = KVR + ROPE
 QWIDE = 256
+WIDE = 640
 HALF = ROPE // 2
 
 rope_base = 50000.0
@@ -84,6 +86,7 @@
         in_specs=[vmem(), vmem()],
         out_specs=[vmem(), vmem()],
         out_shape=[jax.ShapeDtypeStruct((rows, LAT), bf16), jax.ShapeDtypeStruct((rows, 1), jnp.int32)],
+        compiler_params=pltpu.CompilerParams(vmem_limit_bytes=59 * MIB),
         cost_estimate=pl.CostEstimate(flops=8 * rows * 128 * LAT, bytes_accessed=1000000, transcendentals=0),
         name="select",
     )(page_table, jnp.transpose(pool, (1, 2, 0)))
@@ -100,6 +103,7 @@
         in_specs=[vmem(), vmem()],
         out_specs=vmem(),
         out_shape=jax.ShapeDtypeStruct((x.shape[0], w.shape[0]), bf16),
+        compiler_params=pltpu.CompilerParams(vmem_limit_bytes=8 * MIB),
         cost_estimate=pl.CostEstimate(flops=2 * x.size * w.shape[0], bytes_accessed=2 * (x.size + w.size),
                                       transcendentals=0),
         name="project",
@@ -112,7 +116,8 @@
     return jnp.cos(angles), jnp.sin(angles)
 
 
-def query_kernel(length_ref, frequency_ref, ql_ref, wq_hbm, out_ref, wq_ref, sems):
+def query_kernel(length_ref, frequency_ref, ql_ref, wq_hbm, out_ref, done_ref, wq_ref, sems):
+    done_ref[...] = jnp.zeros_like(done_ref)
     heads, _, tokens = out_ref.shape
     pair_width = 2 * (NOPE + ROPE)
     copies = []
@@ -144,13 +149,16 @@
     return pl.pallas_call(
         query_kernel,
         in_specs=[smem(), vmem(), vmem(), hbm()],
-        out_specs=vmem(),
-        out_shape=jax.ShapeDtypeStruct((heads, QWIDE, tokens), bf16),
+        out_specs=[vmem(), vmem()],
+        out_shape=[
+            jax.ShapeDtypeStruct((heads, QWIDE, tokens), bf16),
+            jax.ShapeDtypeStruct((8, 128), f32),
+        ],
         scratch_shapes=[
             pltpu.VMEM((heads // 2, rank, 2 * (NOPE + ROPE)), bf16),
             pltpu.SemaphoreType.DMA((heads // 2,)),
         ],
-        compiler_params=pltpu.CompilerParams(vmem_limit_bytes=24 * MIB),
+        compiler_params=pltpu.CompilerParams(vmem_limit_bytes=56 * MIB),
         cost_estimate=pl.CostEstimate(flops=2 * tokens * rank * heads * 192, bytes_accessed=6 * MIB, transcendentals=0),
         name="queries",
     )(prefix_len, frequency, q_latent, w_q_b)
@@ -177,12 +185,13 @@
         in_specs=[vmem(), vmem()],
         out_specs=[vmem()] * 4,
         out_shape=[jax.ShapeDtypeStruct((rows, LAT), f32)] + [jax.ShapeDtypeStruct((rows, LAT), bf16)] * 3,
+        compiler_params=pltpu.CompilerParams(vmem_limit_bytes=4 * MIB),
         cost_estimate=pl.CostEstimate(flops=a.size, bytes_accessed=8 * a.size, transcendentals=0),
         name="combine",
     )(a, b)
 
 
-def finish_kernel(length_ref, frequency_ref, own_ref, a_ref, b_ref, c_ref, gain_ref, _, out_ref, share_ref):
+def finish_kernel(length_ref, frequency_ref, own_ref, a_ref, b_ref, c_ref, gain_ref, out_ref, share_ref):
     total = (own_ref[...] + a_ref[...].astype(f32)) + (b_ref[...].astype(f32) + c_ref[...].astype(f32))
     rows = total.shape[0]
     nope = total[:, :KVR]
@@ -201,16 +210,17 @@
     share_ref[...] = out_ref[pl.ds(pl.multiple_of(core * half, half), half), :]
 
 
-def finish(prefix_len, frequency, own, a, b, c, gain, earlier):
+def finish(prefix_len, frequency, own, a, b, c, gain):
     rows = own.shape[0]
     return pl.pallas_call(
         finish_kernel,
-        in_specs=[smem()] + [vmem()] * 6 + [anywhere()],
+        in_specs=[smem()] + [vmem()] * 6,
         out_specs=[vmem(), vmem()],
         out_shape=[jax.ShapeDtypeStruct(own.shape, bf16), jax.ShapeDtypeStruct((rows // 2, LAT), bf16)],
+        compiler_params=pltpu.CompilerParams(vmem_limit_bytes=4 * MIB),
         cost_estimate=pl.CostEstimate(flops=8 * own.size, bytes_accessed=12 * own.size, transcendentals=0),
         name="finish",
-    )(prefix_len, frequency, own, a, b, c, gain, earlier)
+    )(prefix_len, frequency, own, a, b, c, gain)
 
 
 def address_kernel(owner_ref, *refs):
@@ -233,6 +243,7 @@
         in_specs=[smem()] + [vmem()] * 4,
         out_specs=vmem(),
         out_shape=jax.ShapeDtypeStruct((8, rows, LAT), bf16),
+        compiler_params=pltpu.CompilerParams(vmem_limit_bytes=4 * MIB),
         cost_estimate=pl.CostEstimate(flops=1000, bytes_accessed=20 * rows * LAT, transcendentals=0),
         name="address",
     )(decode_owner, *shares)
@@ -256,45 +267,74 @@
         out_specs=vmem(),
         out_shape=jax.ShapeDtypeStruct((rows, LAT), bf16),
         scratch_shapes=[pltpu.SemaphoreType.DMA],
+        compiler_params=pltpu.CompilerParams(vmem_limit_bytes=4 * MIB),
         cost_estimate=pl.CostEstimate(flops=1000, bytes_accessed=4 * rows * LAT, transcendentals=0),
         name="pick",
     )(decode_owner, arrived, earlier)
 
 
-def after(x, token):
-    return pl.pallas_call(
-        lambda x_ref, token_ref, out_ref: None,
-        in_specs=[anywhere(), anywhere()],
-        out_specs=anywhere(),
+def copies_kernel(x_ref, _, __, out_ref):
+    x = x_ref[...]
+    for i in range(out_ref.shape[0]):
+        out_ref[i, :, :LAT] = x
+        out_ref[i, :, LAT:] = jnp.zeros((x.shape[0], WIDE - LAT), bf16)
+
+
+def four_copies(x, *tokens):
+    return pl.pallas_call(
+        copies_kernel,
+        in_specs=[vmem(), anywhere(), anywhere()],
+        out_specs=vmem(),
+        out_shape=jax.ShapeDtypeStruct((4, x.shape[0], WIDE), x.dtype),
+        compiler_params=pltpu.CompilerParams(vmem_limit_bytes=8 * MIB),
+        cost_estimate=pl.CostEstimate(flops=0, bytes_accessed=10 * x.size, transcendentals=0),
+        name="four_copies",
+    )(x, *tokens)
+
+
+def again_kernel(x_ref, *refs):
+    out_ref, sems = refs[-2:]
+    copies = [pltpu.make_async_copy(x_ref.at[i], out_ref.at[i], sems.at[i]) for i in range(out_ref.shape[0])]
+    for copy in copies:
+        copy.start()
+    for copy in copies:
+        copy.wait()
+
+
+def again(x, *tokens):
+    return pl.pallas_call(
+        again_kernel,
+        in_specs=[anywhere()] * (1 + len(tokens)),
+        out_specs=hbm(),
         out_shape=jax.ShapeDtypeStruct(x.shape, x.dtype),
-        input_output_aliases={0: 0},
-        cost_estimate=pl.CostEstimate(flops=0, bytes_accessed=0, transcendentals=0),
-        name="after",
-    )(x, token)
-
-
-def attention_kernel(turns, length_ref, pos_ref, qt_ref, wk_hbm, wv_hbm, cached_ref, *refs):
+        scratch_shapes=[pltpu.SemaphoreType.DMA((x.shape[0],))],
+        compiler_params=pltpu.CompilerParams(vmem_limit_bytes=4 * MIB),
+        cost_estimate=pl.CostEstimate(flops=0, bytes_accessed=4 * x.size, transcendentals=0),
+        name="again",
+    )(x, *tokens)
+
+
+def attention_kernel(turns, length_ref, pos_ref, qt_ref, wk_hbm, wv_hbm, same_ref, other_ref, *refs):
     refs = list(refs)
     new_refs = [refs.pop(0) for _ in turns]
-    out_ref, tails, keys, values, scores, weights, landed, fresh, wk_ref, wv_ref, sems, w_sems = refs
+    out_ref, tails, keys, values, scores, weights, landed, fresh, turned, wk_ref, wv_ref, wv_turned, sems, w_sems = refs
     heads, _, tokens = qt_ref.shape
     rows = pos_ref.shape[0]
-    blocks = landed.shape[0]
+    blocks = 8
     tiles = blocks + 1
     tensor = lax.axis_index("tensor")
     length = length_ref[lax.axis_index("group")]
+    core = lax.rem(tensor, 2)
     ups = []
     for pair in range(heads // 2):
         columns = pl.ds(pair * 256, 256)
         for i, (source, target) in enumerate(((wk_hbm, wk_ref), (wv_hbm, wv_ref))):
-            copy = pltpu.make_async_copy(source.at[:, columns], target.at[:, columns], w_sems.at[2 * pair + i])
-            copy.start()
-            ups.append(copy)
+            ups.append(pltpu.make_async_copy(source.at[:, columns], target.at[:, columns], w_sems.at[2 * pair + i]))
     copies = []
     for b in range(blocks):
-        copy = pltpu.make_async_copy(cached_ref.at[pl.ds(b * rows, rows), :], landed.at[b], sems.at[b])
+        copies.append(pltpu.make_async_copy((same_ref if b < 4 else other_ref).at[b % 4], landed.at[b], sems.at[b]))
+    for copy in ups[:2] + copies:
         copy.start()
-        copies.append(copy)
     latents = [landed.at[b] for b in range(blocks)] + [fresh]
     causal = []
     for b, turn in enumerate(turns):
@@ -309,25 +349,31 @@
         here = slice(j * rows, (j + 1) * rows)
         if j < blocks:
             copies[j].wait()
-            out_of_range = jnp.logical_and(pos_ref[...] >= length - 4 * j, lane == 0)
+            source = 2 * (j % 4) + (core if j < 4 else 1 - core)
+            out_of_range = jnp.logical_and(pos_ref[...] >= length - 4 * source, lane == 0)
             tails[here, ROPE:] = jnp.where(out_of_range, masked_value, 0.0).astype(bf16)
         else:
             tails[here, ROPE:] = jnp.zeros((rows, 128 - ROPE), bf16)
         tails[here, :ROPE] = latents[j][:, KVR:LAT]
+        turned[:, here] = latents[j][:, :KVR].T
+
+    def await_weights(pair):
+        columns = slice(pair * 256, (pair + 1) * 256)
+        for copy in ups[2 * pair:2 * pair + 2]:
+            copy.wait()
+        wv_turned[columns, :] = wv_ref[:, columns].T
 
     def project_up(pair, j):
         here = slice(j * rows, (j + 1) * rows)
         nope = latents[j][:, :KVR]
         columns = slice(pair * 256, (pair + 1) * 256)
         k = jnp.dot(nope, wk_ref[:, columns], preferred_element_type=f32).astype(bf16)
-        v = lax.dot_general(
-            wv_ref[:, columns], nope, (((0,), (1,)), ((), ())), preferred_element_type=f32
-        ).astype(bf16)
+        v = jnp.dot(wv_turned[columns, :], turned[:, here], preferred_element_type=f32).astype(bf16)
         for i in range(2):
             slot = 2 * (pair % 2) + i
             keys[slot, here, :NOPE] = k[:, i * NOPE:(i + 1) * NOPE]
             keys[slot, here, NOPE:] = tails[here, :]
-            values[slot, :, here] = v[i * VDIM:(i + 1) * VDIM]
+            values[2 * (pair % 3) + i, :, here] = v[i * VDIM:(i + 1) * VDIM]
 
     def score(h, j):
         here = slice(j * rows, (j + 1) * rows)
@@ -343,12 +389,18 @@
         weights[h % 2, here] = p.astype(bf16)
         return jnp.sum(p, axis=0, keepdims=True)
 
+    def gather_values(h, norm):
+        acc = jnp.dot(values[2 * (h // 2 % 3) + h % 2], weights[h % 2], preferred_element_type=f32)
+        out_ref[:, h * VDIM:(h + 1) * VDIM] = (acc / norm).T.astype(bf16)
+
     order = [blocks] + list(range(blocks))
     tops = []
-    for copy in ups[:2]:
-        copy.wait()
-    for j in order:
+    await_weights(0)
+    for i, j in enumerate(order):
         stage(j)
+        if i == 3:
+            for copy in ups[2:]:
+                copy.start()
         project_up(0, j)
         tops.append(score(0, j))
     for h in range(heads):
@@ -356,47 +408,49 @@
         tops = []
         norms = []
         if h % 2 == 0 and h + 2 < heads:
-            for copy in ups[h + 2:h + 4]:
-                copy.wait()
+            await_weights(h // 2 + 1)
         for i, j in enumerate(order):
             if h // 2 * 2 + 2 < heads and i % 2 == h % 2:
                 project_up(h // 2 + 1, j)
             if h + 1 < heads:
                 tops.append(score(h + 1, j))
             norms.append(weigh(h, j, top))
+            if i == 2 and h > 0:
+                gather_values(h - 1, norm)
         norm = functools.reduce(jnp.add, norms)
-        acc = jnp.dot(values[h % 4], weights[h % 2], preferred_element_type=f32)
-        out_ref[:, h * VDIM:(h + 1) * VDIM] = (acc / norm).T.astype(bf16)
+    gather_values(heads - 1, norm)
 
 
 def attention(prefix_len, pos, qt, w_key_up, w_value_up, cached, turns, new_blocks):
     heads, _, tokens = qt.shape
     rows = pos.shape[0]
-    blocks = cached.shape[0] // rows
+    blocks = 8
     total = rows * (blocks + 1)
     return pl.pallas_call(
         functools.partial(attention_kernel, turns),
-        in_specs=[smem()] + [vmem()] * 2 + [hbm()] * 3 + [vmem()] * len(new_blocks),
+        in_specs=[smem()] + [vmem()] * 2 + [hbm()] * 4 + [vmem()] * len(new_blocks),
         out_specs=vmem(),
         out_shape=jax.ShapeDtypeStruct((tokens, heads * VDIM), bf16),
         scratch_shapes=[
             pltpu.VMEM((total, 128), bf16),
             pltpu.VMEM((4, total, QWIDE), bf16),
-            pltpu.VMEM((4, VDIM, total), bf16),
+            pltpu.VMEM((6, VDIM, total), bf16),
             pltpu.VMEM((2, total, tokens), f32),
             pltpu.VMEM((2, total, tokens), bf16),
-            pltpu.VMEM((blocks, rows, LAT), bf16),
+            pltpu.VMEM((blocks, rows, WIDE), bf16),
             pltpu.VMEM((rows, LAT), bf16),
+            pltpu.VMEM((KVR, total), bf16),
             pltpu.VMEM(w_key_up.shape, bf16),
             pltpu.VMEM(w_value_up.shape, bf16),
+            pltpu.VMEM(w_value_up.shape[::-1], bf16),
             pltpu.SemaphoreType.DMA((blocks,)),
             pltpu.SemaphoreType.DMA((heads,)),
         ],
-        compiler_params=pltpu.CompilerParams(vmem_limit_bytes=32 * MIB),
+        compiler_params=pltpu.CompilerParams(vmem_limit_bytes=58 * MIB),
         cost_estimate=pl.CostEstimate(flops=4 * heads * tokens * total * 512, bytes_accessed=4 * MIB,
                                       transcendentals=heads * tokens * total),
         name="attention",
-    )(prefix_len, pos, qt, w_key_up, w_value_up, cached, *new_blocks)
+    )(prefix_len, pos, qt, w_key_up, w_value_up, *cached, *new_blocks)
 
 
 def shards(
@@ -426,8 +480,9 @@
     incoming = lax.all_to_all(outgoing, "group", split_axis=0, concat_axis=0, tiled=True)
     own_block = incoming.reshape(pos.shape[0], LAT)
 
-    frequency = (rope_base ** (-2.0 * jnp.arange(HALF, dtype=f32) / ROPE))[:, None]
-    qt = make_queries(prefix_len, frequency, q_latent, w_q_b)
+    frequency = jnp.asarray((rope_base ** (-2.0 * np.arange(HALF) / ROPE)).astype(np.float32)[:, None])
+
+    qt, queried = make_queries(prefix_len, frequency, q_latent, w_q_b)
 
     partial_sum = project(hidden, w_kv_a.T)
     partner_sum = tensor_permute(partial_sum, other)
@@ -435,7 +490,7 @@
     from_down = tensor_permute(to_up, up)
     from_up = tensor_permute(to_down, down)
     from_far = tensor_permute(to_far, far)
-    latent, share = finish(prefix_len, frequency, own, from_down, from_up, from_far, kv_gain[None, :], qt)
+    latent, share = finish(prefix_len, frequency, own, from_down, from_up, from_far, kv_gain[None, :])
     latents = [latent, tensor_permute(latent, up), tensor_permute(latent, down), tensor_permute(latent, far)]
 
     def x_permute(turn):
@@ -445,8 +500,11 @@
     addressed = address(decode_owner, [share, x_permute(1), x_permute(2), x_permute(3)])
     arrived = lax.all_to_all(addressed, "group", 0, 0, tiled=True, axis_index_groups=columns)
 
-    own_block = after(own_block, own)
-    cached = lax.all_gather(own_block, "tensor", axis=0, tiled=True)
+    same_core = lax.all_to_all(
+        four_copies(own_block, latent, queried), "tensor", 0, 0, tiled=True, axis_index_groups=[[0, 2, 4, 6], [1, 3, 5, 7]]
+    )
+    same_core = again(same_core, addressed, *latents[1:])
+    cached = [same_core, tensor_permute(same_core, other)]
     attn_out = attention(prefix_len, pos, qt, w_key_up, w_value_up, cached, (0, 3, 1, 2), latents)
     decode_pages = pick(decode_owner, arrived, attn_out)
     return (attn_out, decode_pages)

time: 99.7 us -> 88.2 us (0.88)
  the two profiles are of different devices: /device:TPU:16 before, /device:TPU:1 now
where the time goes in v3:
time: 88.2 us; the launch traced here: 87.6 us
  starting transfers between devices  38.7 us (44%)
  Pallas kernels  32.9 us (37%)
  waiting for transfers between devices  11 us (12%)
  local copies, waits for them, and re-layouts  4.02 us (5%)
  between operations  1.01 us (1%)
    pallas_call x1, Pallas kernels, attention(): pl.pallas_call(functools.partial(attention_kernel, turns), in_specs=[smem...  18.5 us
    ppermute x8, starting transfers between devices, tensor_permute(): return lax.ppermute(x, 'tensor', [(i, step(i)) for i in range(8)])  12.5 us
    all_to_all x1, starting transfers between devices, shards(): lax.all_to_all(outgoing, 'group', split_axis=0, concat_axis=0, tiled=True)  11.9 us
    ppermute x8, waiting for transfers between devices, tensor_permute(): return lax.ppermute(x, 'tensor', [(i, step(i)) for i in range(8)])  7.05 us
    all_to_all x1, starting transfers between devices, shards(): lax.all_to_all(addressed, 'group', 0, 0, tiled=True, axis_index_groups=co...  6.7 us
    pallas_call x1, Pallas kernels, make_queries(): pl.pallas_call(query_kernel, in_specs=[smem(), vmem(), vmem(), hbm()], ou...  6.15 us
    unnamed x28, local copies, waits for them, and re-layouts  4.02 us
    ppermute x3, starting transfers between devices, x_permute(): lax.ppermute(share, 'group', [(i, i // 4 * 4 + (i + turn) % 4) for i in r...  3.95 us
  transfers between devices with their start and end apart: 14, of which 6 were waited for; matrix products, arithmetic and copies ran while one was open for 0% of the time, Pallas kernels for 31%

profile of v3, /device:TPU:1, one launch (start us, length us, event | category | flops | bytes accessed | tf_op | source)
XLA Modules:
  0.0 87.6 jit_solution(17997851388655270945)
XLA Ops:
  0.6 2.5 %select.1 = (bf16[256,576]{1,0:T(8,128)(2,1)}, s32[256,1]{1,0:T(8,128)}) custom-call(s32[32,64]{1,0:T(8,128)} %table_ref.1, bf16[4,576,128]{2,1,0:T(8,128)(2,1)} %bitcast.8), custom_call_target="tpu_custom_call" | custom-call | flops 150994944 | bytes 1000000 | tf_op jit(solution)/shard_map/select/pallas_call | solution.py:84
  3.2 11.9 %all-to-all-start = ((bf16[32,8,576]{2,1,0:T(8,128)(2,1)}), bf16[32,8,576]{2,1,0:T(8,128)(2,1)S(1)}, u32[]{:S(2)}, u32[]{:S(2)}) async-start(bf16[32,8,576]{2,1,0:T(8,128)(2,1)} %bitcast.9), calls=%async_computation | async-start | bytes 655360 | tf_op jit(solution)/shard_map/all_to_all | solution.py:480
  15.1 1.0 %copy-done.3 = bf16[256,896]{1,0:T(8,128)(2,1)S(1)} copy-done((bf16[256,896]{1,0:T(8,128)(2,1)S(1)}, bf16[256,896]{1,0:T(8,128)(2,1)}, u32[]{:S(2)}) %copy-start.3) | copy-done | bytes 458776
  16.1 0.6 project.1.a_ref
  16.7 1.0 %collective-permute-start = (bf16[256,576]{1,0:T(8,128)(2,1)S(1)}, bf16[256,576]{1,0:T(8,128)(2,1)S(1)}, u32[]{:S(2)}, u32[]{:S(2)}) collective-permute-start(bf16[256,576]{1,0:T(8,128)(2,1)S(1)} %project.1.a_ref), channel_id=1, source_target_pairs={{0,1},{1,0},{2,3},{3,2},{4,5},{5,4},{6,7},{7,6},{8,9},{9,8},{10,11... | collective-permute-start | bytes 884744 | tf_op jit(solution)/shard_map/ppermute | solution.py:471
  17.7 1.3 %collective-permute-done.b_ref = bf16[256,576]{1,0:T(8,128)(2,1)S(1)} collective-permute-done((bf16[256,576]{1,0:T(8,128)(2,1)S(1)}, bf16[256,576]{1,0:T(8,128)(2,1)S(1)}, u32[]{:S(2)}, u32[]{:S(2)}) %collective-permute-start) | collective-permute-done | bytes 294944 | tf_op jit(solution)/shard_map/ppermute | solution.py:471
  19.1 1.4 %collective-permute-start.1 = (bf16[64,576]{1,0:T(8,128)(2,1)S(1)}, bf16[64,576]{1,0:T(8,128)(2,1)S(1)}, u32[]{:S(2)}, u32[]{:S(2)}) collective-permute-start(bf16[64,576]{1,0:T(8,128)(2,1)S(1)} %get-tuple-element.16), channel_id=1, source_target_pairs={{0,2},{1,3},{2,4},{3,5},{4,6},{5,7},{6,0},{7,1},{8,10},{9,11},{10,... | collective-permute-start | bytes 221192 | tf_op jit(solution)/shard_map/ppermute | solution.py:471
  20.4 1.5 %collective-permute-start.2 = (bf16[64,576]{1,0:T(8,128)(2,1)S(1)}, bf16[64,576]{1,0:T(8,128)(2,1)S(1)}, u32[]{:S(2)}, u32[]{:S(2)}) collective-permute-start(bf16[64,576]{1,0:T(8,128)(2,1)S(1)} %get-tuple-element.17), channel_id=1, source_target_pairs={{0,6},{1,7},{2,0},{3,1},{4,2},{5,3},{6,4},{7,5},{8,14},{9,15},{10,... | collective-permute-start | bytes 221192 | tf_op jit(solution)/shard_map/ppermute | solution.py:471
  22.0 1.6 %collective-permute-start.3 = (bf16[64,576]{1,0:T(8,128)(2,1)S(1)}, bf16[64,576]{1,0:T(8,128)(2,1)S(1)}, u32[]{:S(2)}, u32[]{:S(2)}) collective-permute-start(bf16[64,576]{1,0:T(8,128)(2,1)S(1)} %get-tuple-element.18), channel_id=1, source_target_pairs={{0,4},{1,5},{2,6},{3,7},{4,0},{5,1},{6,2},{7,3},{8,12},{9,13},{10,... | collective-permute-start | bytes 221192 | tf_op jit(solution)/shard_map/ppermute | solution.py:471
  23.5 6.2 %queries.1 = (bf16[8,256,256]{2,1,0:T(8,128)(2,1)}, f32[8,128]{1,0:T(8,128)}) custom-call(s32[32]{0:T(128)} %length_ref.5, f32[32,1]{1,0:T(8,128)} %constant.2.clone.frequency_ref, bf16[256,1536]{1,0:T(8,128)(2,1)} %ql_ref.1, bf16[1536,1536]{1,0:T(8,128)(2,1)} %wq_hbm.1), custom_call_target="tpu_custom_call" | custom-call | flops 1207959552 | bytes 6291456 | tf_op jit(solution)/shard_map/queries/pallas_call | solution.py:149
  29.7 0.8 finish.1
  30.6 0.7 copy-done.9
  31.3 1.2 %four_copies.1 = bf16[4,256,640]{2,1,0:T(8,128)(2,1)} custom-call(bf16[256,576]{1,0:T(8,128)(2,1)S(1)} %bitcast.5, bf16[64,576]{1,0:T(8,128)(2,1)S(1)} %get-tuple-element.19._.refs_0_, f32[8,128]{1,0:T(8,128)S(1)} %copy-done.9), custom_call_target="tpu_custom_call" | custom-call | bytes 1474560 | tf_op jit(solution)/shard_map/four_copies/pallas_call | solution.py:284
  32.5 3.7 %all-to-all-start.1 = ((bf16[4,256,640]{2,1,0:T(8,128)(2,1)}), bf16[4,256,640]{2,1,0:T(8,128)(2,1)S(1)}, u32[]{:S(2)}, u32[]{:S(2)}) async-start(bf16[4,256,640]{2,1,0:T(8,128)(2,1)} %four_copies.1), calls=%async_computation.1 | async-start | bytes 2621440 | tf_op jit(solution)/shard_map/all_to_all | solution.py:503
  36.2 2.8 %collective-permute-start.6 = (bf16[32,576]{1,0:T(8,128)(2,1)S(1)}, bf16[32,576]{1,0:T(8,128)(2,1)S(1)}, u32[]{:S(2)}, u32[]{:S(2)}) collective-permute-start(bf16[32,576]{1,0:T(8,128)(2,1)S(1)} %get-tuple-element.21.refs_0_), channel_id=1, source_target_pairs={{0,24},{8,0},{16,8},{24,16},{32,56},{40,32},{48,40},{56,48},{64,88... | collective-permute-start | bytes 110600 | tf_op jit(solution)/shard_map/ppermute | solution.py:497
  39.0 2.9 %collective-permute-start.9 = (bf16[64,576]{1,0:T(8,128)(2,1)S(1)}, bf16[64,576]{1,0:T(8,128)(2,1)S(1)}, u32[]{:S(2)}, u32[]{:S(2)}) collective-permute-start(bf16[64,576]{1,0:T(8,128)(2,1)S(1)} %get-tuple-element.19._.refs_0_), channel_id=1, source_target_pairs={{0,4},{1,5},{2,6},{3,7},{4,0},{5,1},{6,2},{7,3},{8,12},{9,13},{10,... | collective-permute-start | bytes 221192 | tf_op jit(solution)/shard_map/ppermute | solution.py:471
  41.8 0.9 %collective-permute-start.8 = (bf16[64,576]{1,0:T(8,128)(2,1)S(1)}, bf16[64,576]{1,0:T(8,128)(2,1)S(1)}, u32[]{:S(2)}, u32[]{:S(2)}) collective-permute-start(bf16[64,576]{1,0:T(8,128)(2,1)S(1)} %get-tuple-element.19._.refs_0_), channel_id=1, source_target_pairs={{0,6},{1,7},{2,0},{3,1},{4,2},{5,3},{6,4},{7,5},{8,14},{9,15},{10,... | collective-permute-start | bytes 221192 | tf_op jit(solution)/shard_map/ppermute | solution.py:471
  42.7 0.6 collective-permute-start.7
  43.3 0.6 collective-permute-start.5
  43.9 0.6 collective-permute-start.4
  44.4 3.2 %collective-permute-done.5.refs_2_ = bf16[32,576]{1,0:T(8,128)(2,1)S(1)} collective-permute-done((bf16[32,576]{1,0:T(8,128)(2,1)S(1)}, bf16[32,576]{1,0:T(8,128)(2,1)S(1)}, u32[]{:S(2)}, u32[]{:S(2)}) %collective-permute-start.5) | collective-permute-done | bytes 36896 | tf_op jit(solution)/shard_map/ppermute | solution.py:497
  47.7 0.7 collective-permute-done.4.refs_1_
  48.4 1.3 %address.1.refs_0_ = bf16[8,32,576]{2,1,0:T(8,128)(2,1)} custom-call(s32[32]{0:T(128)S(1)} %copy-done.12, bf16[32,576]{1,0:T(8,128)(2,1)S(1)} %get-tuple-element.21.refs_0_, bf16[32,576]{1,0:T(8,128)(2,1)S(1)} %collective-permute-done.4.refs_1_, bf16[32,576]{1,0:T(8,128)(2,1)S(1)} %collective-permute-done.5.refs_2_, ...), custom_call_target="tpu_custom_call" | custom-call | flops 1000 | bytes 368640 | tf_op jit(solution)/shard_map/address/pallas_call | solution.py:241
  49.7 4.9 %collective-permute-done.9.refs_3_ = bf16[64,576]{1,0:T(8,128)(2,1)S(1)} collective-permute-done((bf16[64,576]{1,0:T(8,128)(2,1)S(1)}, bf16[64,576]{1,0:T(8,128)(2,1)S(1)}, u32[]{:S(2)}, u32[]{:S(2)}) %collective-permute-start.9) | collective-permute-done | bytes 73760 | tf_op jit(solution)/shard_map/ppermute | solution.py:471
  54.9 0.6 collective-permute-done.7.refs_1_
  55.5 0.4 again.1.same_ref
  56.2 2.7 %collective-permute-start.10 = (bf16[4,256,640]{2,1,0:T(8,128)(2,1)S(1)}, bf16[4,256,640]{2,1,0:T(8,128)(2,1)S(1)}, u32[]{:S(2)}, u32[]{:S(2)}) collective-permute-start(bf16[4,256,640]{2,1,0:T(8,128)(2,1)S(1)} %again.1.same_ref), channel_id=1, source_target_pairs={{0,1},{1,0},{2,3},{3,2},{4,5},{5,4},{6,7},{7,6},{8,9},{9,8},{10,11... | collective-permute-start | bytes 3932168 | tf_op jit(solution)/shard_map/ppermute | solution.py:471
  58.8 6.7 %all-to-all-start.2 = ((bf16[8,32,576]{2,1,0:T(8,128)(2,1)}), bf16[8,32,576]{2,1,0:T(8,128)(2,1)S(1)}, u32[]{:S(2)}, u32[]{:S(2)}) async-start(bf16[8,32,576]{2,1,0:T(8,128)(2,1)} %address.1.refs_0_), calls=%async_computation.2 | async-start | bytes 655360 | tf_op jit(solution)/shard_map/all_to_all | solution.py:501
  65.6 1.1 %copy-done.13 = bf16[4,256,640]{2,1,0:T(8,128)(2,1)} copy-done((bf16[4,256,640]{2,1,0:T(8,128)(2,1)}, bf16[4,256,640]{2,1,0:T(8,128)(2,1)S(1)}, u32[]{:S(2)}) %copy-start.13) | copy-done | bytes 1310744
  66.6 18.5 %attention.1._ = bf16[256,1024]{1,0:T(8,128)(2,1)} custom-call(s32[32]{0:T(128)} %length_ref.5, s32[256,1]{1,0:T(8,128)} %get-tuple-element.12.pos_ref, bf16[8,256,256]{2,1,0:T(8,128)(2,1)} %get-tuple-element.13.qt_ref, bf16[512,1024]{1,0:T(8,128)(2,1)} %wk_hbm.1, bf16[512,1024]{1,0:T(8,128)(2,1)} %wv_hbm.1, bf16[4,256,640]{2,1,0:T(8,128)(2,1)} %copy-done, ...), custom_call_target="tpu_custom_call" | custom-call | flops 9663676416 | bytes 4194304 | tf_op jit(solution)/shard_map/attention/pallas_call | solution.py:429
  85.1 1.0 %copy-done.2 = bf16[256,1024]{1,0:T(8,128)(2,1)S(1)} copy-done((bf16[256,1024]{1,0:T(8,128)(2,1)S(1)}, bf16[256,1024]{1,0:T(8,128)(2,1)}, u32[]{:S(2)}) %copy-start.2) | copy-done | bytes 524312
  86.2 1.3 %pick.1 = bf16[32,576]{1,0:T(8,128)(2,1)} custom-call(s32[32]{0:T(128)S(1)} %copy-done.12, bf16[8,32,576]{2,1,0:T(8,128)(2,1)S(1)} %all-to-all-done.2.in_ref, bf16[256,1024]{1,0:T(8,128)(2,1)S(1)} %copy-done.2), custom_call_target="tpu_custom_call" | custom-call | flops 1000 | bytes 73728 | tf_op jit(solution)/shard_map/pick/pallas_call | solution.py:264
  (34 shorter events, 0.5 us)
Async XLA Ops:
  0.6 14.4 %copy-start.1 = (bf16[896,576]{0,1:T(8,128)(2,1)S(1)}, bf16[896,576]{0,1:T(8,128)(2,1)}, u32[]{:S(2)}) copy-start(bf16[896,576]{0,1:T(8,128)(2,1)} %param.13) | copy-start | bytes 3096580
  3.2 27.3 %all-to-all-start = ((bf16[32,8,576]{2,1,0:T(8,128)(2,1)}), bf16[32,8,576]{2,1,0:T(8,128)(2,1)S(1)}, u32[]{:S(2)}, u32[]{:S(2)}) async-start(bf16[32,8,576]{2,1,0:T(8,128)(2,1)} %bitcast.9), calls=%async_computation | async-start | bytes 655360 | tf_op jit(solution)/shard_map/all_to_all | solution.py:480
  15.1 1.0 %copy-start.3 = (bf16[256,896]{1,0:T(8,128)(2,1)S(1)}, bf16[256,896]{1,0:T(8,128)(2,1)}, u32[]{:S(2)}) copy-start(bf16[256,896]{1,0:T(8,128)(2,1)} %x_ref.1) | copy-start | bytes 1376260
  16.7 2.3 %collective-permute-start = (bf16[256,576]{1,0:T(8,128)(2,1)S(1)}, bf16[256,576]{1,0:T(8,128)(2,1)S(1)}, u32[]{:S(2)}, u32[]{:S(2)}) collective-permute-start(bf16[256,576]{1,0:T(8,128)(2,1)S(1)} %project.1.a_ref), channel_id=1, source_target_pairs={{0,1},{1,0},{2,3},{3,2},{4,5},{5,4},{6,7},{7,6},{8,9},{9,8},{10,11... | collective-permute-start | bytes 884744 | tf_op jit(solution)/shard_map/ppermute | solution.py:471
  19.1 10.6 %collective-permute-start.1 = (bf16[64,576]{1,0:T(8,128)(2,1)S(1)}, bf16[64,576]{1,0:T(8,128)(2,1)S(1)}, u32[]{:S(2)}, u32[]{:S(2)}) collective-permute-start(bf16[64,576]{1,0:T(8,128)(2,1)S(1)} %get-tuple-element.16), channel_id=1, source_target_pairs={{0,2},{1,3},{2,4},{3,5},{4,6},{5,7},{6,0},{7,1},{8,10},{9,11},{10,... | collective-permute-start | bytes 221192 | tf_op jit(solution)/shard_map/ppermute | solution.py:471
  20.4 9.3 %collective-permute-start.2 = (bf16[64,576]{1,0:T(8,128)(2,1)S(1)}, bf16[64,576]{1,0:T(8,128)(2,1)S(1)}, u32[]{:S(2)}, u32[]{:S(2)}) collective-permute-start(bf16[64,576]{1,0:T(8,128)(2,1)S(1)} %get-tuple-element.17), channel_id=1, source_target_pairs={{0,6},{1,7},{2,0},{3,1},{4,2},{5,3},{6,4},{7,5},{8,14},{9,15},{10,... | collective-permute-start | bytes 221192 | tf_op jit(solution)/shard_map/ppermute | solution.py:471
  22.0 7.8 %copy-start.8 = (f32[32,1]{1,0:T(8,128)S(1)}, f32[32,1]{1,0:T(8,128)}, u32[]{:S(2)}) copy-start(f32[32,1]{1,0:T(8,128)} %constant.2.clone.frequency_ref) | copy-start | bytes 388
  22.0 7.8 %copy-start.10 = (f32[512]{0:T(512)S(1)}, f32[512]{0:T(512)}, u32[]{:S(2)}) copy-start(f32[512]{0:T(512)} %param.14) | copy-start | bytes 6148
  22.0 7.8 %copy-start.11 = (s32[32]{0:T(128)S(1)}, s32[32]{0:T(128)}, u32[]{:S(2)}) copy-start(s32[32]{0:T(128)} %length_ref.5) | copy-start | bytes 388
  22.0 7.7 %collective-permute-start.3 = (bf16[64,576]{1,0:T(8,128)(2,1)S(1)}, bf16[64,576]{1,0:T(8,128)(2,1)S(1)}, u32[]{:S(2)}, u32[]{:S(2)}) collective-permute-start(bf16[64,576]{1,0:T(8,128)(2,1)S(1)} %get-tuple-element.18), channel_id=1, source_target_pairs={{0,4},{1,5},{2,6},{3,7},{4,0},{5,1},{6,2},{7,3},{8,12},{9,13},{10,... | collective-permute-start | bytes 221192 | tf_op jit(solution)/shard_map/ppermute | solution.py:471
  30.5 12.2 %copy-start.7 = (bf16[64,576]{1,0:T(8,128)(2,1)}, bf16[64,576]{1,0:T(8,128)(2,1)S(1)}, u32[]{:S(2)}) copy-start(bf16[64,576]{1,0:T(8,128)(2,1)S(1)} %get-tuple-element.19._.refs_0_) | copy-start | bytes 221188
  30.5 0.7 copy-start.9
  32.5 15.9 %copy-start.12 = (s32[32]{0:T(128)S(1)}, s32[32]{0:T(128)}, u32[]{:S(2)}) copy-start(s32[32]{0:T(128)} %owner_ref.3) | copy-start | bytes 388
  32.5 23.0 %all-to-all-start.1 = ((bf16[4,256,640]{2,1,0:T(8,128)(2,1)}), bf16[4,256,640]{2,1,0:T(8,128)(2,1)S(1)}, u32[]{:S(2)}, u32[]{:S(2)}) async-start(bf16[4,256,640]{2,1,0:T(8,128)(2,1)} %four_copies.1), calls=%async_computation.1 | async-start | bytes 2621440 | tf_op jit(solution)/shard_map/all_to_all | solution.py:503
  36.2 7.7 %collective-permute-start.6 = (bf16[32,576]{1,0:T(8,128)(2,1)S(1)}, bf16[32,576]{1,0:T(8,128)(2,1)S(1)}, u32[]{:S(2)}, u32[]{:S(2)}) collective-permute-start(bf16[32,576]{1,0:T(8,128)(2,1)S(1)} %get-tuple-element.21.refs_0_), channel_id=1, source_target_pairs={{0,24},{8,0},{16,8},{24,16},{32,56},{40,32},{48,40},{56,48},{64,88... | collective-permute-start | bytes 110600 | tf_op jit(solution)/shard_map/ppermute | solution.py:497
  39.0 15.7 %collective-permute-start.9 = (bf16[64,576]{1,0:T(8,128)(2,1)S(1)}, bf16[64,576]{1,0:T(8,128)(2,1)S(1)}, u32[]{:S(2)}, u32[]{:S(2)}) collective-permute-start(bf16[64,576]{1,0:T(8,128)(2,1)S(1)} %get-tuple-element.19._.refs_0_), channel_id=1, source_target_pairs={{0,4},{1,5},{2,6},{3,7},{4,0},{5,1},{6,2},{7,3},{8,12},{9,13},{10,... | collective-permute-start | bytes 221192 | tf_op jit(solution)/shard_map/ppermute | solution.py:471
  41.8 13.1 %collective-permute-start.8 = (bf16[64,576]{1,0:T(8,128)(2,1)S(1)}, bf16[64,576]{1,0:T(8,128)(2,1)S(1)}, u32[]{:S(2)}, u32[]{:S(2)}) collective-permute-start(bf16[64,576]{1,0:T(8,128)(2,1)S(1)} %get-tuple-element.19._.refs_0_), channel_id=1, source_target_pairs={{0,6},{1,7},{2,0},{3,1},{4,2},{5,3},{6,4},{7,5},{8,14},{9,15},{10,... | collective-permute-start | bytes 221192 | tf_op jit(solution)/shard_map/ppermute | solution.py:471
  42.7 12.8 %collective-permute-start.7 = (bf16[64,576]{1,0:T(8,128)(2,1)S(1)}, bf16[64,576]{1,0:T(8,128)(2,1)S(1)}, u32[]{:S(2)}, u32[]{:S(2)}) collective-permute-start(bf16[64,576]{1,0:T(8,128)(2,1)S(1)} %get-tuple-element.19._.refs_0_), channel_id=1, source_target_pairs={{0,2},{1,3},{2,4},{3,5},{4,6},{5,7},{6,0},{7,1},{8,10},{9,11},{10,... | collective-permute-start | bytes 221192 | tf_op jit(solution)/shard_map/ppermute | solution.py:471
  43.3 4.4 %collective-permute-start.5 = (bf16[32,576]{1,0:T(8,128)(2,1)S(1)}, bf16[32,576]{1,0:T(8,128)(2,1)S(1)}, u32[]{:S(2)}, u32[]{:S(2)}) collective-permute-start(bf16[32,576]{1,0:T(8,128)(2,1)S(1)} %get-tuple-element.21.refs_0_), channel_id=1, source_target_pairs={{0,16},{8,24},{16,0},{24,8},{32,48},{40,56},{48,32},{56,40},{64,80... | collective-permute-start | bytes 110600 | tf_op jit(solution)/shard_map/ppermute | solution.py:497
  43.9 4.5 %collective-permute-start.4 = (bf16[32,576]{1,0:T(8,128)(2,1)S(1)}, bf16[32,576]{1,0:T(8,128)(2,1)S(1)}, u32[]{:S(2)}, u32[]{:S(2)}) collective-permute-start(bf16[32,576]{1,0:T(8,128)(2,1)S(1)} %get-tuple-element.21.refs_0_), channel_id=1, source_target_pairs={{0,8},{8,16},{16,24},{24,0},{32,40},{40,48},{48,56},{56,32},{64,72... | collective-permute-start | bytes 110600 | tf_op jit(solution)/shard_map/ppermute | solution.py:497
  54.6 1.3 %copy-start.4 = (bf16[64,576]{1,0:T(8,128)(2,1)}, bf16[64,576]{1,0:T(8,128)(2,1)S(1)}, u32[]{:S(2)}) copy-start(bf16[64,576]{1,0:T(8,128)(2,1)S(1)} %collective-permute-done.9.refs_3_) | copy-start | bytes 221188
  54.9 1.1 %copy-start.5 = (bf16[64,576]{1,0:T(8,128)(2,1)}, bf16[64,576]{1,0:T(8,128)(2,1)S(1)}, u32[]{:S(2)}) copy-start(bf16[64,576]{1,0:T(8,128)(2,1)S(1)} %collective-permute-done.8.refs_2_) | copy-start | bytes 221188
  55.5 0.6 copy-start.6
  56.2 9.4 %copy-start = (bf16[4,256,640]{2,1,0:T(8,128)(2,1)}, bf16[4,256,640]{2,1,0:T(8,128)(2,1)S(1)}, u32[]{:S(2)}) copy-start(bf16[4,256,640]{2,1,0:T(8,128)(2,1)S(1)} %again.1.same_ref) | copy-start | bytes 3932164
  56.2 9.4 %collective-permute-start.10 = (bf16[4,256,640]{2,1,0:T(8,128)(2,1)S(1)}, bf16[4,256,640]{2,1,0:T(8,128)(2,1)S(1)}, u32[]{:S(2)}, u32[]{:S(2)}) collective-permute-start(bf16[4,256,640]{2,1,0:T(8,128)(2,1)S(1)} %again.1.same_ref), channel_id=1, source_target_pairs={{0,1},{1,0},{2,3},{3,2},{4,5},{5,4},{6,7},{7,6},{8,9},{9,8},{10,11... | collective-permute-start | bytes 3932168 | tf_op jit(solution)/shard_map/ppermute | solution.py:471
  58.8 26.3 %all-to-all-start.2 = ((bf16[8,32,576]{2,1,0:T(8,128)(2,1)}), bf16[8,32,576]{2,1,0:T(8,128)(2,1)S(1)}, u32[]{:S(2)}, u32[]{:S(2)}) async-start(bf16[8,32,576]{2,1,0:T(8,128)(2,1)} %address.1.refs_0_), calls=%async_computation.2 | async-start | bytes 655360 | tf_op jit(solution)/shard_map/all_to_all | solution.py:501
  65.5 1.1 %copy-start.13 = (bf16[4,256,640]{2,1,0:T(8,128)(2,1)}, bf16[4,256,640]{2,1,0:T(8,128)(2,1)S(1)}, u32[]{:S(2)}) copy-start(bf16[4,256,640]{2,1,0:T(8,128)(2,1)S(1)} %collective-permute-done.10.other_ref) | copy-start | bytes 3932164
  85.1 1.0 %copy-start.2 = (bf16[256,1024]{1,0:T(8,128)(2,1)S(1)}, bf16[256,1024]{1,0:T(8,128)(2,1)}, u32[]{:S(2)}) copy-start(bf16[256,1024]{1,0:T(8,128)(2,1)} %attention.1._) | copy-start | bytes 1572868

commit v4 on v3

--- a/solution.py
+++ b/solution.py
@@ -317,7 +317,8 @@
 def attention_kernel(turns, length_ref, pos_ref, qt_ref, wk_hbm, wv_hbm, same_ref, other_ref, *refs):
     refs = list(refs)
     new_refs = [refs.pop(0) for _ in turns]
-    out_ref, tails, keys, values, scores, weights, landed, fresh, turned, wk_ref, wv_ref, wv_turned, sems, w_sems = refs
+    out_ref, done_ref, tails, keys, values, scores, weights, fresh, turned, wk_ref, wv_ref, wv_turned, w_sems = refs
+    done_ref[...] = jnp.zeros_like(done_ref)
     heads, _, tokens = qt_ref.shape
     rows = pos_ref.shape[0]
     blocks = 8
@@ -330,12 +331,9 @@
         columns = pl.ds(pair * 256, 256)
         for i, (source, target) in enumerate(((wk_hbm, wk_ref), (wv_hbm, wv_ref))):
             ups.append(pltpu.make_async_copy(source.at[:, columns], target.at[:, columns], w_sems.at[2 * pair + i]))
-    copies = []
-    for b in range(blocks):
-        copies.append(pltpu.make_async_copy((same_ref if b < 4 else other_ref).at[b % 4], landed.at[b], sems.at[b]))
-    for copy in ups[:2] + copies:
+    for copy in ups:
         copy.start()
-    latents = [landed.at[b] for b in range(blocks)] + [fresh]
+    latents = [ref.at[y] for ref in (same_ref, other_ref) for y in range(4)] + [fresh]
     causal = []
     for b, turn in enumerate(turns):
         n = new_refs[b].shape[0]
@@ -348,7 +346,6 @@
     def stage(j):
         here = slice(j * rows, (j + 1) * rows)
         if j < blocks:
-            copies[j].wait()
             source = 2 * (j % 4) + (core if j < 4 else 1 - core)
             out_of_range = jnp.logical_and(pos_ref[...] >= length - 4 * source, lane == 0)
             tails[here, ROPE:] = jnp.where(out_of_range, masked_value, 0.0).astype(bf16)
@@ -396,11 +393,8 @@
     order = [blocks] + list(range(blocks))
     tops = []
     await_weights(0)
-    for i, j in enumerate(order):
+    for j in order:
         stage(j)
-        if i == 3:
-            for copy in ups[2:]:
-                copy.start()
         project_up(0, j)
         tops.append(score(0, j))
     for h in range(heads):
@@ -428,25 +422,26 @@
     total = rows * (blocks + 1)
     return pl.pallas_call(
         functools.partial(attention_kernel, turns),
-        in_specs=[smem()] + [vmem()] * 2 + [hbm()] * 4 + [vmem()] * len(new_blocks),
-        out_specs=vmem(),
-        out_shape=jax.ShapeDtypeStruct((tokens, heads * VDIM), bf16),
+        in_specs=[smem()] + [vmem()] * 2 + [hbm()] * 2 + [vmem()] * (2 + len(new_blocks)),
+        out_specs=[vmem(), vmem()],
+        out_shape=[
+            jax.ShapeDtypeStruct((tokens, heads * VDIM), bf16),
+            jax.ShapeDtypeStruct((8, 128), f32),
+        ],
         scratch_shapes=[
             pltpu.VMEM((total, 128), bf16),
             pltpu.VMEM((4, total, QWIDE), bf16),
             pltpu.VMEM((6, VDIM, total), bf16),
             pltpu.VMEM((2, total, tokens), f32),
             pltpu.VMEM((2, total, tokens), bf16),
-            pltpu.VMEM((blocks, rows, WIDE), bf16),
             pltpu.VMEM((rows, LAT), bf16),
             pltpu.VMEM((KVR, total), bf16),
             pltpu.VMEM(w_key_up.shape, bf16),
             pltpu.VMEM(w_value_up.shape, bf16),
             pltpu.VMEM(w_value_up.shape[::-1], bf16),
-            pltpu.SemaphoreType.DMA((blocks,)),
             pltpu.SemaphoreType.DMA((heads,)),
         ],
-        compiler_params=pltpu.CompilerParams(vmem_limit_bytes=58 * MIB),
+        compiler_params=pltpu.CompilerParams(vmem_limit_bytes=32 * MIB),
         cost_estimate=pl.CostEstimate(flops=4 * heads * tokens * total * 512, bytes_accessed=4 * MIB,
                                       transcendentals=heads * tokens * total),
         name="attention",
@@ -505,8 +500,8 @@
     )
     same_core = again(same_core, addressed, *latents[1:])
     cached = [same_core, tensor_permute(same_core, other)]
-    attn_out = attention(prefix_len, pos, qt, w_key_up, w_value_up, cached, (0, 3, 1, 2), latents)
-    decode_pages = pick(decode_owner, arrived, attn_out)
+    attn_out, attended = attention(prefix_len, pos, qt, w_key_up, w_value_up, cached, (0, 3, 1, 2), latents)
+    decode_pages = pick(decode_owner, arrived, attended)
     return (attn_out, decode_pages)
 
 

time: 88.2 us -> 87.2 us (0.989)
  Pallas kernels: 32.9 us -> 30.5 us
  local copies, waits for them, and re-layouts: 4.02 us -> 5.39 us
    pallas_call x1, Pallas kernels: 18.5 us -> 16 us  [attention(): pl.pallas_call(functools.partial(attention_kernel, turns), in_specs=[smem...]
    unnamed x28 -> x22, local copies, waits for them, and re-layouts: 4.02 us -> 5.39 us
  transfers between devices with their start and end apart: 14 -> 14, of which waited for: 6 -> 6; matrix products, arithmetic and copies ran while one was open for 0% -> 0% of each run, Pallas kernels for 31% -> 29%
where the time goes in v4:
time: 87.2 us; the launch traced here: 86.6 us
  starting transfers between devices  38.8 us (44%)
  Pallas kernels  30.5 us (35%)
  waiting for transfers between devices  11 us (13%)
  local copies, waits for them, and re-layouts  5.39 us (6%)
  between operations  0.97 us (1%)
    pallas_call x1, Pallas kernels, attention(): pl.pallas_call(functools.partial(attention_kernel, turns), in_specs=[smem...  16 us
    ppermute x8, starting transfers between devices, tensor_permute(): return lax.ppermute(x, 'tensor', [(i, step(i)) for i in range(8)])  12.6 us
    all_to_all x1, starting transfers between devices, shards(): lax.all_to_all(outgoing, 'group', split_axis=0, concat_axis=0, tiled=True)  11.9 us
    ppermute x8, waiting for transfers between devices, tensor_permute(): return lax.ppermute(x, 'tensor', [(i, step(i)) for i in range(8)])  7.03 us
    all_to_all x1, starting transfers between devices, shards(): lax.all_to_all(addressed, 'group', 0, 0, tiled=True, axis_index_groups=co...  6.7 us
    pallas_call x1, Pallas kernels, make_queries(): pl.pallas_call(query_kernel, in_specs=[smem(), vmem(), vmem(), hbm()], ou...  6.18 us
    unnamed x22, local copies, waits for them, and re-layouts  5.39 us
    ppermute x3, starting transfers between devices, x_permute(): lax.ppermute(share, 'group', [(i, i // 4 * 4 + (i + turn) % 4) for i in r...  3.95 us
  transfers between devices with their start and end apart: 14, of which 6 were waited for; matrix products, arithmetic and copies ran while one was open for 0% of the time, Pallas kernels for 29%

profile of v4, /device:TPU:1, one launch (start us, length us, event | category | flops | bytes accessed | tf_op | source)
XLA Modules:
  0.0 86.6 jit_solution(11590449043514414237)
XLA Ops:
  0.6 2.5 %select.1 = (bf16[256,576]{1,0:T(8,128)(2,1)}, s32[256,1]{1,0:T(8,128)}) custom-call(s32[32,64]{1,0:T(8,128)} %table_ref.1, bf16[4,576,128]{2,1,0:T(8,128)(2,1)} %bitcast.8), custom_call_target="tpu_custom_call" | custom-call | flops 150994944 | bytes 1000000 | tf_op jit(solution)/shard_map/select/pallas_call | solution.py:84
  3.2 11.9 %all-to-all-start = ((bf16[32,8,576]{2,1,0:T(8,128)(2,1)}), bf16[32,8,576]{2,1,0:T(8,128)(2,1)S(1)}, u32[]{:S(2)}, u32[]{:S(2)}) async-start(bf16[32,8,576]{2,1,0:T(8,128)(2,1)} %bitcast.9), calls=%async_computation | async-start | bytes 655360 | tf_op jit(solution)/shard_map/all_to_all | solution.py:475
  15.1 1.0 %copy-done.1 = bf16[256,896]{1,0:T(8,128)(2,1)S(1)} copy-done((bf16[256,896]{1,0:T(8,128)(2,1)S(1)}, bf16[256,896]{1,0:T(8,128)(2,1)}, u32[]{:S(2)}) %copy-start.1) | copy-done | bytes 458776
  16.1 0.6 project.1.a_ref
  16.7 1.0 %collective-permute-start = (bf16[256,576]{1,0:T(8,128)(2,1)S(1)}, bf16[256,576]{1,0:T(8,128)(2,1)S(1)}, u32[]{:S(2)}, u32[]{:S(2)}) collective-permute-start(bf16[256,576]{1,0:T(8,128)(2,1)S(1)} %project.1.a_ref), channel_id=1, source_target_pairs={{0,1},{1,0},{2,3},{3,2},{4,5},{5,4},{6,7},{7,6},{8,9},{9,8},{10,11... | collective-permute-start | bytes 884744 | tf_op jit(solution)/shard_map/ppermute | solution.py:466
  17.7 1.3 %collective-permute-done.b_ref = bf16[256,576]{1,0:T(8,128)(2,1)S(1)} collective-permute-done((bf16[256,576]{1,0:T(8,128)(2,1)S(1)}, bf16[256,576]{1,0:T(8,128)(2,1)S(1)}, u32[]{:S(2)}, u32[]{:S(2)}) %collective-permute-start) | collective-permute-done | bytes 294944 | tf_op jit(solution)/shard_map/ppermute | solution.py:466
  19.1 1.4 %collective-permute-start.1 = (bf16[64,576]{1,0:T(8,128)(2,1)S(1)}, bf16[64,576]{1,0:T(8,128)(2,1)S(1)}, u32[]{:S(2)}, u32[]{:S(2)}) collective-permute-start(bf16[64,576]{1,0:T(8,128)(2,1)S(1)} %get-tuple-element.18), channel_id=1, source_target_pairs={{0,2},{1,3},{2,4},{3,5},{4,6},{5,7},{6,0},{7,1},{8,10},{9,11},{10,... | collective-permute-start | bytes 221192 | tf_op jit(solution)/shard_map/ppermute | solution.py:466
  20.4 1.5 %collective-permute-start.2 = (bf16[64,576]{1,0:T(8,128)(2,1)S(1)}, bf16[64,576]{1,0:T(8,128)(2,1)S(1)}, u32[]{:S(2)}, u32[]{:S(2)}) collective-permute-start(bf16[64,576]{1,0:T(8,128)(2,1)S(1)} %get-tuple-element.19), channel_id=1, source_target_pairs={{0,6},{1,7},{2,0},{3,1},{4,2},{5,3},{6,4},{7,5},{8,14},{9,15},{10,... | collective-permute-start | bytes 221192 | tf_op jit(solution)/shard_map/ppermute | solution.py:466
  22.0 1.6 %collective-permute-start.3 = (bf16[64,576]{1,0:T(8,128)(2,1)S(1)}, bf16[64,576]{1,0:T(8,128)(2,1)S(1)}, u32[]{:S(2)}, u32[]{:S(2)}) collective-permute-start(bf16[64,576]{1,0:T(8,128)(2,1)S(1)} %get-tuple-element.20), channel_id=1, source_target_pairs={{0,4},{1,5},{2,6},{3,7},{4,0},{5,1},{6,2},{7,3},{8,12},{9,13},{10,... | collective-permute-start | bytes 221192 | tf_op jit(solution)/shard_map/ppermute | solution.py:466
  23.5 6.2 %queries.1 = (bf16[8,256,256]{2,1,0:T(8,128)(2,1)}, f32[8,128]{1,0:T(8,128)}) custom-call(s32[32]{0:T(128)} %length_ref.5, f32[32,1]{1,0:T(8,128)} %constant.2.clone.frequency_ref, bf16[256,1536]{1,0:T(8,128)(2,1)} %ql_ref.1, bf16[1536,1536]{1,0:T(8,128)(2,1)} %wq_hbm.1), custom_call_target="tpu_custom_call" | custom-call | flops 1207959552 | bytes 6291456 | tf_op jit(solution)/shard_map/queries/pallas_call | solution.py:149
  29.8 0.8 finish.1
  30.6 0.7 copy-done.3
  31.2 1.2 %four_copies.1 = bf16[4,256,640]{2,1,0:T(8,128)(2,1)} custom-call(bf16[256,576]{1,0:T(8,128)(2,1)S(1)} %bitcast.5, bf16[64,576]{1,0:T(8,128)(2,1)S(1)} %get-tuple-element.21._.refs_0_, f32[8,128]{1,0:T(8,128)S(1)} %copy-done.3), custom_call_target="tpu_custom_call" | custom-call | bytes 1474560 | tf_op jit(solution)/shard_map/four_copies/pallas_call | solution.py:284
  32.5 3.7 %all-to-all-start.1 = ((bf16[4,256,640]{2,1,0:T(8,128)(2,1)}), bf16[4,256,640]{2,1,0:T(8,128)(2,1)S(1)}, u32[]{:S(2)}, u32[]{:S(2)}) async-start(bf16[4,256,640]{2,1,0:T(8,128)(2,1)} %four_copies.1), calls=%async_computation.1 | async-start | bytes 2621440 | tf_op jit(solution)/shard_map/all_to_all | solution.py:498
  36.1 2.8 %collective-permute-start.6 = (bf16[32,576]{1,0:T(8,128)(2,1)S(1)}, bf16[32,576]{1,0:T(8,128)(2,1)S(1)}, u32[]{:S(2)}, u32[]{:S(2)}) collective-permute-start(bf16[32,576]{1,0:T(8,128)(2,1)S(1)} %get-tuple-element.23.refs_0_), channel_id=1, source_target_pairs={{0,24},{8,0},{16,8},{24,16},{32,56},{40,32},{48,40},{56,48},{64,88... | collective-permute-start | bytes 110600 | tf_op jit(solution)/shard_map/ppermute | solution.py:492
  39.0 2.9 %collective-permute-start.9 = (bf16[64,576]{1,0:T(8,128)(2,1)S(1)}, bf16[64,576]{1,0:T(8,128)(2,1)S(1)}, u32[]{:S(2)}, u32[]{:S(2)}) collective-permute-start(bf16[64,576]{1,0:T(8,128)(2,1)S(1)} %get-tuple-element.21._.refs_0_), channel_id=1, source_target_pairs={{0,4},{1,5},{2,6},{3,7},{4,0},{5,1},{6,2},{7,3},{8,12},{9,13},{10,... | collective-permute-start | bytes 221192 | tf_op jit(solution)/shard_map/ppermute | solution.py:466
  41.8 0.9 %collective-permute-start.8 = (bf16[64,576]{1,0:T(8,128)(2,1)S(1)}, bf16[64,576]{1,0:T(8,128)(2,1)S(1)}, u32[]{:S(2)}, u32[]{:S(2)}) collective-permute-start(bf16[64,576]{1,0:T(8,128)(2,1)S(1)} %get-tuple-element.21._.refs_0_), channel_id=1, source_target_pairs={{0,6},{1,7},{2,0},{3,1},{4,2},{5,3},{6,4},{7,5},{8,14},{9,15},{10,... | collective-permute-start | bytes 221192 | tf_op jit(solution)/shard_map/ppermute | solution.py:466
  42.7 0.6 collective-permute-start.7
  43.3 0.6 collective-permute-start.5
  43.9 0.6 collective-permute-start.4
  44.4 3.2 %collective-permute-done.5.refs_2_ = bf16[32,576]{1,0:T(8,128)(2,1)S(1)} collective-permute-done((bf16[32,576]{1,0:T(8,128)(2,1)S(1)}, bf16[32,576]{1,0:T(8,128)(2,1)S(1)}, u32[]{:S(2)}, u32[]{:S(2)}) %collective-permute-start.5) | collective-permute-done | bytes 36896 | tf_op jit(solution)/shard_map/ppermute | solution.py:492
  47.6 0.7 collective-permute-done.4.refs_1_
  48.4 1.4 %address.1.refs_0_ = bf16[8,32,576]{2,1,0:T(8,128)(2,1)} custom-call(s32[32]{0:T(128)S(1)} %copy-done.6, bf16[32,576]{1,0:T(8,128)(2,1)S(1)} %get-tuple-element.23.refs_0_, bf16[32,576]{1,0:T(8,128)(2,1)S(1)} %collective-permute-done.4.refs_1_, bf16[32,576]{1,0:T(8,128)(2,1)S(1)} %collective-permute-done.5.refs_2_, ...), custom_call_target="tpu_custom_call" | custom-call | flops 1000 | bytes 368640 | tf_op jit(solution)/shard_map/address/pallas_call | solution.py:241
  49.7 4.9 %collective-permute-done.9.refs_3_ = bf16[64,576]{1,0:T(8,128)(2,1)S(1)} collective-permute-done((bf16[64,576]{1,0:T(8,128)(2,1)S(1)}, bf16[64,576]{1,0:T(8,128)(2,1)S(1)}, u32[]{:S(2)}, u32[]{:S(2)}) %collective-permute-start.9) | collective-permute-done | bytes 73760 | tf_op jit(solution)/shard_map/ppermute | solution.py:466
  54.9 0.6 collective-permute-done.7.refs_1_
  56.0 2.8 %collective-permute-start.10 = (bf16[4,256,640]{2,1,0:T(8,128)(2,1)S(1)}, bf16[4,256,640]{2,1,0:T(8,128)(2,1)}, u32[]{:S(2)}, u32[]{:S(2)}) collective-permute-start(bf16[4,256,640]{2,1,0:T(8,128)(2,1)S(1)} %again.1.same_ref), channel_id=1, source_target_pairs={{0,1},{1,0},{2,3},{3,2},{4,5},{5,4},{6,7},{7,6},{8,9},{9,8},{10,11... | collective-permute-start | bytes 3932168 | tf_op jit(solution)/shard_map/ppermute | solution.py:466
  58.7 6.7 %all-to-all-start.2 = ((bf16[8,32,576]{2,1,0:T(8,128)(2,1)}), bf16[8,32,576]{2,1,0:T(8,128)(2,1)S(1)}, u32[]{:S(2)}, u32[]{:S(2)}) async-start(bf16[8,32,576]{2,1,0:T(8,128)(2,1)} %address.1.refs_0_), calls=%async_computation.2 | async-start | bytes 655360 | tf_op jit(solution)/shard_map/all_to_all | solution.py:496
  65.5 1.2 %copy-done.7 = bf16[512,1024]{1,0:T(8,128)(2,1)S(1)} copy-done((bf16[512,1024]{1,0:T(8,128)(2,1)S(1)}, bf16[512,1024]{1,0:T(8,128)(2,1)}, u32[]{:S(2)}) %copy-start.7) | copy-done | bytes 1048600
  66.7 1.2 %copy-done.8 = bf16[512,1024]{1,0:T(8,128)(2,1)S(1)} copy-done((bf16[512,1024]{1,0:T(8,128)(2,1)S(1)}, bf16[512,1024]{1,0:T(8,128)(2,1)}, u32[]{:S(2)}) %copy-start.8) | copy-done | bytes 1048600
  67.9 1.2 %copy-done.9 = bf16[8,256,256]{2,1,0:T(8,128)(2,1)S(1)} copy-done((bf16[8,256,256]{2,1,0:T(8,128)(2,1)S(1)}, bf16[8,256,256]{2,1,0:T(8,128)(2,1)}, u32[]{:S(2)}) %copy-start.9) | copy-done | bytes 1048600
  69.1 16.0 %attention.1 = (bf16[256,1024]{1,0:T(8,128)(2,1)}, f32[8,128]{1,0:T(8,128)S(1)}) custom-call(s32[32]{0:T(128)S(1)} %copy-done.5, s32[256,1]{1,0:T(8,128)S(1)} %copy-done.10, bf16[8,256,256]{2,1,0:T(8,128)(2,1)S(1)} %copy-done.9, bf16[512,1024]{1,0:T(8,128)(2,1)S(1)} %copy-done.7, bf16[512,1024]{1,0:T(8,128)(2,1)S(1)} %copy-done.8, ...), custom_call_target="tpu_custom_call" | custom-call | flops 9663676416 | bytes 4194304 | tf_op jit(solution)/shard_map/attention/pallas_call | solution.py:423
  85.2 1.3 %pick.1 = bf16[32,576]{1,0:T(8,128)(2,1)} custom-call(s32[32]{0:T(128)S(1)} %copy-done.6, bf16[8,32,576]{2,1,0:T(8,128)(2,1)S(1)} %all-to-all-done.2.in_ref, f32[8,128]{1,0:T(8,128)S(1)} %get-tuple-element.25._), custom_call_target="tpu_custom_call" | custom-call | flops 1000 | bytes 73728 | tf_op jit(solution)/shard_map/pick/pallas_call | solution.py:264
  (28 shorter events, 0.8 us)
Async XLA Ops:
  0.6 14.4 %copy-start = (bf16[896,576]{0,1:T(8,128)(2,1)S(1)}, bf16[896,576]{0,1:T(8,128)(2,1)}, u32[]{:S(2)}) copy-start(bf16[896,576]{0,1:T(8,128)(2,1)} %param.13) | copy-start | bytes 3096580
  3.2 27.4 %all-to-all-start = ((bf16[32,8,576]{2,1,0:T(8,128)(2,1)}), bf16[32,8,576]{2,1,0:T(8,128)(2,1)S(1)}, u32[]{:S(2)}, u32[]{:S(2)}) async-start(bf16[32,8,576]{2,1,0:T(8,128)(2,1)} %bitcast.9), calls=%async_computation | async-start | bytes 655360 | tf_op jit(solution)/shard_map/all_to_all | solution.py:475
  15.1 1.0 %copy-start.1 = (bf16[256,896]{1,0:T(8,128)(2,1)S(1)}, bf16[256,896]{1,0:T(8,128)(2,1)}, u32[]{:S(2)}) copy-start(bf16[256,896]{1,0:T(8,128)(2,1)} %x_ref.1) | copy-start | bytes 1376260
  16.7 2.3 %collective-permute-start = (bf16[256,576]{1,0:T(8,128)(2,1)S(1)}, bf16[256,576]{1,0:T(8,128)(2,1)S(1)}, u32[]{:S(2)}, u32[]{:S(2)}) collective-permute-start(bf16[256,576]{1,0:T(8,128)(2,1)S(1)} %project.1.a_ref), channel_id=1, source_target_pairs={{0,1},{1,0},{2,3},{3,2},{4,5},{5,4},{6,7},{7,6},{8,9},{9,8},{10,11... | collective-permute-start | bytes 884744 | tf_op jit(solution)/shard_map/ppermute | solution.py:466
  19.1 10.7 %collective-permute-start.1 = (bf16[64,576]{1,0:T(8,128)(2,1)S(1)}, bf16[64,576]{1,0:T(8,128)(2,1)S(1)}, u32[]{:S(2)}, u32[]{:S(2)}) collective-permute-start(bf16[64,576]{1,0:T(8,128)(2,1)S(1)} %get-tuple-element.18), channel_id=1, source_target_pairs={{0,2},{1,3},{2,4},{3,5},{4,6},{5,7},{6,0},{7,1},{8,10},{9,11},{10,... | collective-permute-start | bytes 221192 | tf_op jit(solution)/shard_map/ppermute | solution.py:466
  20.4 9.3 %collective-permute-start.2 = (bf16[64,576]{1,0:T(8,128)(2,1)S(1)}, bf16[64,576]{1,0:T(8,128)(2,1)S(1)}, u32[]{:S(2)}, u32[]{:S(2)}) collective-permute-start(bf16[64,576]{1,0:T(8,128)(2,1)S(1)} %get-tuple-element.19), channel_id=1, source_target_pairs={{0,6},{1,7},{2,0},{3,1},{4,2},{5,3},{6,4},{7,5},{8,14},{9,15},{10,... | collective-permute-start | bytes 221192 | tf_op jit(solution)/shard_map/ppermute | solution.py:466
  22.0 7.8 %copy-start.2 = (f32[32,1]{1,0:T(8,128)S(1)}, f32[32,1]{1,0:T(8,128)}, u32[]{:S(2)}) copy-start(f32[32,1]{1,0:T(8,128)} %constant.2.clone.frequency_ref) | copy-start | bytes 388
  22.0 7.8 %copy-start.4 = (f32[512]{0:T(512)S(1)}, f32[512]{0:T(512)}, u32[]{:S(2)}) copy-start(f32[512]{0:T(512)} %param.14) | copy-start | bytes 6148
  22.0 7.8 %copy-start.5 = (s32[32]{0:T(128)S(1)}, s32[32]{0:T(128)}, u32[]{:S(2)}) copy-start(s32[32]{0:T(128)} %length_ref.5) | copy-start | bytes 388
  22.0 7.8 %collective-permute-start.3 = (bf16[64,576]{1,0:T(8,128)(2,1)S(1)}, bf16[64,576]{1,0:T(8,128)(2,1)S(1)}, u32[]{:S(2)}, u32[]{:S(2)}) collective-permute-start(bf16[64,576]{1,0:T(8,128)(2,1)S(1)} %get-tuple-element.20), channel_id=1, source_target_pairs={{0,4},{1,5},{2,6},{3,7},{4,0},{5,1},{6,2},{7,3},{8,12},{9,13},{10,... | collective-permute-start | bytes 221192 | tf_op jit(solution)/shard_map/ppermute | solution.py:466
  30.6 0.7 copy-start.3
  32.5 15.9 %copy-start.6 = (s32[32]{0:T(128)S(1)}, s32[32]{0:T(128)}, u32[]{:S(2)}) copy-start(s32[32]{0:T(128)} %owner_ref.3) | copy-start | bytes 388
  32.5 23.0 %all-to-all-start.1 = ((bf16[4,256,640]{2,1,0:T(8,128)(2,1)}), bf16[4,256,640]{2,1,0:T(8,128)(2,1)S(1)}, u32[]{:S(2)}, u32[]{:S(2)}) async-start(bf16[4,256,640]{2,1,0:T(8,128)(2,1)} %four_copies.1), calls=%async_computation.1 | async-start | bytes 2621440 | tf_op jit(solution)/shard_map/all_to_all | solution.py:498
  36.1 7.7 %collective-permute-start.6 = (bf16[32,576]{1,0:T(8,128)(2,1)S(1)}, bf16[32,576]{1,0:T(8,128)(2,1)S(1)}, u32[]{:S(2)}, u32[]{:S(2)}) collective-permute-start(bf16[32,576]{1,0:T(8,128)(2,1)S(1)} %get-tuple-element.23.refs_0_), channel_id=1, source_target_pairs={{0,24},{8,0},{16,8},{24,16},{32,56},{40,32},{48,40},{56,48},{64,88... | collective-permute-start | bytes 110600 | tf_op jit(solution)/shard_map/ppermute | solution.py:492
  39.0 15.7 %collective-permute-start.9 = (bf16[64,576]{1,0:T(8,128)(2,1)S(1)}, bf16[64,576]{1,0:T(8,128)(2,1)S(1)}, u32[]{:S(2)}, u32[]{:S(2)}) collective-permute-start(bf16[64,576]{1,0:T(8,128)(2,1)S(1)} %get-tuple-element.21._.refs_0_), channel_id=1, source_target_pairs={{0,4},{1,5},{2,6},{3,7},{4,0},{5,1},{6,2},{7,3},{8,12},{9,13},{10,... | collective-permute-start | bytes 221192 | tf_op jit(solution)/shard_map/ppermute | solution.py:466
  41.8 13.1 %collective-permute-start.8 = (bf16[64,576]{1,0:T(8,128)(2,1)S(1)}, bf16[64,576]{1,0:T(8,128)(2,1)S(1)}, u32[]{:S(2)}, u32[]{:S(2)}) collective-permute-start(bf16[64,576]{1,0:T(8,128)(2,1)S(1)} %get-tuple-element.21._.refs_0_), channel_id=1, source_target_pairs={{0,6},{1,7},{2,0},{3,1},{4,2},{5,3},{6,4},{7,5},{8,14},{9,15},{10,... | collective-permute-start | bytes 221192 | tf_op jit(solution)/shard_map/ppermute | solution.py:466
  42.7 12.8 %collective-permute-start.7 = (bf16[64,576]{1,0:T(8,128)(2,1)S(1)}, bf16[64,576]{1,0:T(8,128)(2,1)S(1)}, u32[]{:S(2)}, u32[]{:S(2)}) collective-permute-start(bf16[64,576]{1,0:T(8,128)(2,1)S(1)} %get-tuple-element.21._.refs_0_), channel_id=1, source_target_pairs={{0,2},{1,3},{2,4},{3,5},{4,6},{5,7},{6,0},{7,1},{8,10},{9,11},{10,... | collective-permute-start | bytes 221192 | tf_op jit(solution)/shard_map/ppermute | solution.py:466
  43.3 4.4 %collective-permute-start.5 = (bf16[32,576]{1,0:T(8,128)(2,1)S(1)}, bf16[32,576]{1,0:T(8,128)(2,1)S(1)}, u32[]{:S(2)}, u32[]{:S(2)}) collective-permute-start(bf16[32,576]{1,0:T(8,128)(2,1)S(1)} %get-tuple-element.23.refs_0_), channel_id=1, source_target_pairs={{0,16},{8,24},{16,0},{24,8},{32,48},{40,56},{48,32},{56,40},{64,80... | collective-permute-start | bytes 110600 | tf_op jit(solution)/shard_map/ppermute | solution.py:492
  43.9 4.5 %collective-permute-start.4 = (bf16[32,576]{1,0:T(8,128)(2,1)S(1)}, bf16[32,576]{1,0:T(8,128)(2,1)S(1)}, u32[]{:S(2)}, u32[]{:S(2)}) collective-permute-start(bf16[32,576]{1,0:T(8,128)(2,1)S(1)} %get-tuple-element.23.refs_0_), channel_id=1, source_target_pairs={{0,8},{8,16},{16,24},{24,0},{32,40},{40,48},{48,56},{56,32},{64,72... | collective-permute-start | bytes 110600 | tf_op jit(solution)/shard_map/ppermute | solution.py:492
  49.7 15.7 %copy-start.10 = (s32[256,1]{1,0:T(8,128)S(1)}, s32[256,1]{1,0:T(8,128)}, u32[]{:S(2)}) copy-start(s32[256,1]{1,0:T(8,128)} %get-tuple-element.14.pos_ref) | copy-start | bytes 3076
  56.0 9.5 %collective-permute-start.10 = (bf16[4,256,640]{2,1,0:T(8,128)(2,1)S(1)}, bf16[4,256,640]{2,1,0:T(8,128)(2,1)}, u32[]{:S(2)}, u32[]{:S(2)}) collective-permute-start(bf16[4,256,640]{2,1,0:T(8,128)(2,1)S(1)} %again.1.same_ref), channel_id=1, source_target_pairs={{0,1},{1,0},{2,3},{3,2},{4,5},{5,4},{6,7},{7,6},{8,9},{9,8},{10,11... | collective-permute-start | bytes 3932168 | tf_op jit(solution)/shard_map/ppermute | solution.py:466
  58.7 26.4 %all-to-all-start.2 = ((bf16[8,32,576]{2,1,0:T(8,128)(2,1)}), bf16[8,32,576]{2,1,0:T(8,128)(2,1)S(1)}, u32[]{:S(2)}, u32[]{:S(2)}) async-start(bf16[8,32,576]{2,1,0:T(8,128)(2,1)} %address.1.refs_0_), calls=%async_computation.2 | async-start | bytes 655360 | tf_op jit(solution)/shard_map/all_to_all | solution.py:496
  65.5 1.2 %copy-start.7 = (bf16[512,1024]{1,0:T(8,128)(2,1)S(1)}, bf16[512,1024]{1,0:T(8,128)(2,1)}, u32[]{:S(2)}) copy-start(bf16[512,1024]{1,0:T(8,128)(2,1)} %wk_hbm.1) | copy-start | bytes 3145732
  66.7 1.2 %copy-start.8 = (bf16[512,1024]{1,0:T(8,128)(2,1)S(1)}, bf16[512,1024]{1,0:T(8,128)(2,1)}, u32[]{:S(2)}) copy-start(bf16[512,1024]{1,0:T(8,128)(2,1)} %wv_hbm.1) | copy-start | bytes 3145732
  67.9 1.2 %copy-start.9 = (bf16[8,256,256]{2,1,0:T(8,128)(2,1)S(1)}, bf16[8,256,256]{2,1,0:T(8,128)(2,1)}, u32[]{:S(2)}) copy-start(bf16[8,256,256]{2,1,0:T(8,128)(2,1)} %get-tuple-element.15.qt_ref) | copy-start | bytes 3145732
